TPU v7x, 256 devices: a whole 4x4x8 slice. The times are simulated.
256 devices in a mesh: row: 8 (over y, core), col: 32 (over z, x).
Axes of the slice: x: 4, y: 4, z: 8, core: 2. Of those that a mesh axis runs over, the one named last changes fastest.
Arguments:
- tokens: bfloat16 [768, 8192], P('col', 'row'), may hold values from -6 to 6
- grad_out: bfloat16 [768, 8192], P('col', 'row'), may hold values from -6 to 6
- w_gate: bfloat16 [8192, 16384], P('row', 'col'), may hold values from -0.125 to 0.125
- w_up: bfloat16 [8192, 16384], P('row', 'col'), may hold values from -0.125 to 0.125
- w_down: bfloat16 [16384, 8192], P('col', 'row'), may hold values from -0.09375 to 0.09375
- block_flags: int32 [64, 128], P('row', 'col'), may hold values from 0 to 1, as said below
- token_order: int32 [768], replicated, may hold values from 0 to 767, each once
Outputs:
- grad_in: bfloat16 [768, 8192], P('col', 'row')
- grad_gate: bfloat16 [8192, 16384], P('row', 'col')
- grad_up: bfloat16 [8192, 16384], P('row', 'col')
- grad_down: bfloat16 [16384, 8192], P('col', 'row')
Inputs may be any that keep to these rules, and one draw needn't show every extreme that they name: `block_flags`: within the tile of blocks of one device (8192 / 8 by 16384 / 32 features) at most 16 flags are 1, and some tile has exactly 16. `token_order`: A permutation of the token rows.
All inputs are finite; a program needn't handle non-finite values.
Results may differ from a plain program's by a relative error of at most 0.034.
Values may be sent and summed in bfloat16 or wider, within the bound.
A program may use at most 128 MiB of HBM per device.

v0:
```python
import jax
import jax.numpy as jnp
from jax import lax
from jax.sharding import PartitionSpec as P


def slot_tables(flag_tile, count):
    nbd, nbf = flag_tile.shape
    flat = flag_tile.reshape(-1)
    slots = jnp.argsort(-flat, stable=True)[:count]
    valid = flat[slots].astype(jnp.float32)
    row_block = slots // nbf
    col_block = slots % nbf
    onehot_d = (row_block[:, None] == jnp.arange(nbd, dtype=jnp.int32)[None, :]).astype(jnp.float32)
    onehot_f = (col_block[:, None] == jnp.arange(nbf, dtype=jnp.int32)[None, :]).astype(jnp.float32)
    return (row_block, col_block, valid, onehot_d, onehot_f)


def swiglu_back(gate, up, hidden_grad):
    sig = jax.nn.sigmoid(gate)
    silu = gate * sig
    hidden = (silu * up).astype(jnp.bfloat16)
    d_up = (hidden_grad * silu).astype(jnp.bfloat16)
    d_gate = (hidden_grad * up * sig * (1.0 + gate * (1.0 - sig))).astype(jnp.bfloat16)
    return (hidden, d_gate, d_up)


def on_device(tokens, grad_out, w_gate, w_up, w_down, block_flags, token_order):
    high = lax.Precision.HIGHEST
    nbd, nbf = block_flags.shape
    width_r, width_c = w_gate.shape
    blk = width_r // nbd
    count = nbd * nbf // 2
    row_block, col_block, valid, onehot_d, onehot_f = slot_tables(block_flags, count)
    keep = valid.astype(jnp.bfloat16)[:, None, None]
    gate_blocks = w_gate.reshape(nbd, blk, nbf, blk)[row_block, :, col_block, :] * keep
    up_blocks = w_up.reshape(nbd, blk, nbf, blk)[row_block, :, col_block, :] * keep
    down_blocks = w_down.reshape(nbf, blk, nbd, blk)[col_block, :, row_block, :] * keep
    x_all, dy_all = (
        lax.all_gather(tokens, "col", axis=0, tiled=True),
        lax.all_gather(grad_out, "col", axis=0, tiled=True),
    )
    dy_all = dy_all[token_order]
    total = x_all.shape[0]
    x_packed = x_all.reshape(total, nbd, blk)[:, row_block, :]
    dy_packed = dy_all.reshape(total, nbd, blk)[:, row_block, :]

    def onto_columns(slot_vals):
        return jnp.einsum("tnj,nf->tfj", slot_vals, onehot_f, precision=high).reshape(
            total, width_c
        )

    gate_part = onto_columns(
        jnp.einsum("tnk,nkj->tnj", x_packed, gate_blocks, preferred_element_type=jnp.float32)
    )
    up_part = onto_columns(
        jnp.einsum("tnk,nkj->tnj", x_packed, up_blocks, preferred_element_type=jnp.float32)
    )
    dh_part = onto_columns(
        jnp.einsum("tnk,njk->tnj", dy_packed, down_blocks, preferred_element_type=jnp.float32)
    )
    gate, up, hidden_grad = (
        lax.psum(gate_part.astype(jnp.bfloat16), "row").astype(jnp.float32),
        lax.psum(up_part.astype(jnp.bfloat16), "row").astype(jnp.float32),
        lax.psum(dh_part.astype(jnp.bfloat16), "row").astype(jnp.float32),
    )
    hidden, d_gate, d_up = swiglu_back(gate, up, hidden_grad)
    hidden_p = hidden.reshape(total, nbf, blk)[:, col_block, :]
    d_gate_p = d_gate.reshape(total, nbf, blk)[:, col_block, :]
    d_up_p = d_up.reshape(total, nbf, blk)[:, col_block, :]
    slot_dx = jnp.einsum("tnj,nkj->tnk", d_gate_p, gate_blocks, preferred_element_type=jnp.float32)
    slot_dx = slot_dx + jnp.einsum(
        "tnj,nkj->tnk", d_up_p, up_blocks, preferred_element_type=jnp.float32
    )
    grad_in = lax.psum_scatter(
        jnp.einsum("tnk,nd->tdk", slot_dx, onehot_d, precision=high)
        .reshape(lax.axis_size("col") * tokens.shape[0], width_r)
        .astype(jnp.bfloat16),
        "col",
        scatter_dimension=0,
        tiled=True,
    )
    placed_d = onehot_d * valid[:, None]
    gate_grad = jnp.einsum("tnk,tnj->nkj", x_packed, d_gate_p, preferred_element_type=jnp.float32)
    up_grad = jnp.einsum("tnk,tnj->nkj", x_packed, d_up_p, preferred_element_type=jnp.float32)
    down_grad = jnp.einsum("tnj,tnk->njk", hidden_p, dy_packed, preferred_element_type=jnp.float32)
    grad_gate = jnp.einsum(
        "nkj,nd,nf->dkfj", gate_grad, placed_d, onehot_f, precision=high
    ).reshape(width_r, width_c)
    grad_up = jnp.einsum("nkj,nd,nf->dkfj", up_grad, placed_d, onehot_f, precision=high).reshape(
        width_r, width_c
    )
    grad_down = jnp.einsum(
        "njk,nd,nf->fjdk", down_grad, placed_d, onehot_f, precision=high
    ).reshape(width_c, width_r)
    return (
        grad_in,
        grad_gate.astype(jnp.bfloat16),
        grad_up.astype(jnp.bfloat16),
        grad_down.astype(jnp.bfloat16),
    )


def solution(mesh):
    return jax.shard_map(
        on_device,
        mesh=mesh,
        in_specs=(
            P("col", "row"),
            P("col", "row"),
            P("row", "col"),
            P("row", "col"),
            P("col", "row"),
            P("row", "col"),
            P(),
        ),
        out_specs=(P("col", "row"), P("row", "col"), P("row", "col"), P("col", "row")),
        check_vma=False,
    )
```

profile of v0, /device:TPU:8, one launch (start us, length us, event | category | flops | bytes accessed | tf_op | source)
XLA Modules:
  0.0 571.9 jit_solution(34326645666630358)
XLA Ops:
  20.1 70.6 %all-gather.5.cloned.1.call-done = bf16[768,1024]{1,0:T(8,128)(2,1)} async-done(((bf16[24,1024]{1,0:T(8,128)(2,1)}), bf16[768,1024]{1,0:T(8,128)(2,1)}) %all-gather.5.cloned.1.call-update) | async-done | bytes 1572880 | tf_op jit(solution)/shard_map/all_gather | solution.py:40
  94.0 74.0 %all-gather.3.cloned.1.call-done = bf16[768,1024]{1,0:T(8,128)(2,1)} async-done(((bf16[24,1024]{1,0:T(8,128)(2,1)}), bf16[768,1024]{1,0:T(8,128)(2,1)}) %all-gather.3.cloned.1.call-update) | async-done | bytes 1572880 | tf_op jit(solution)/shard_map/all_gather | solution.py:41
  168.0 5.4 gather_fusion.3
  174.9 2.6 gather_fusion.6
  177.4 4.0 gather_fusion.4
  181.4 5.7 %fusion.19 = f32[768,16,128]{0,2,1:T(8,128)} fusion(bf16[16,768,128]{2,1,0:T(8,128)(2,1)} %gather_fusion.4, bf16[16,128,128]{2,1,0:T(8,128)(2,1)} %gather_fusion.2, bf16[16]{0:T(256)(128)(2,1)S(1)} %get-tuple-element.30), kind=kOutput, calls=%fused_computation.30 | convolution fusion | flops 402915328 | bytes 9961504 | tf_op jit(solution)/shard_map/tnk,njk->tnj/dot_general | solution.py:60
  187.2 6.6 %copy.54 = f32[768,16,128]{2,1,0:T(8,128)} copy(f32[768,16,128]{0,2,1:T(8,128)} %fusion.19) | data formatting | bytes 12582912 | tf_op jit(solution)/shard_map/tnk,njk->tnj/transpose | solution.py:60
  193.8 6.1 %fusion.41 = bf16[768,4,128]{2,1,0:T(4,128)(2,1)} fusion(f32[768,16,128]{2,1,0:T(8,128)} %copy.54, s32[16]{0:T(128)S(1)} %get-tuple-element.22), kind=kOutput, calls=%fused_computation.59 | convolution fusion | flops 75890752 | bytes 7077952 | tf_op jit(solution)/shard_map/tnj,nf->tfj/dot_general | solution.py:49
  199.9 2.2 copy.88
  202.1 5.2 fusion.22
  207.2 6.7 %copy.61 = f32[768,16,128]{2,1,0:T(8,128)} copy(f32[768,16,128]{0,2,1:T(8,128)} %fusion.22) | data formatting | bytes 12582912 | tf_op jit(solution)/shard_map/tnk,nkj->tnj/transpose | solution.py:57
  214.0 6.1 %fusion.42 = bf16[768,4,128]{2,1,0:T(4,128)(2,1)} fusion(f32[768,16,128]{2,1,0:T(8,128)} %copy.61, s32[16]{0:T(128)S(1)} %get-tuple-element.22), kind=kOutput, calls=%fused_computation.60 | convolution fusion | flops 75890752 | bytes 7077952 | tf_op jit(solution)/shard_map/tnj,nf->tfj/dot_general | solution.py:49
  220.1 2.2 copy.91
  222.3 5.1 fusion.25
  227.5 6.6 %copy.64 = f32[768,16,128]{2,1,0:T(8,128)} copy(f32[768,16,128]{0,2,1:T(8,128)} %fusion.25) | data formatting | bytes 12582912 | tf_op jit(solution)/shard_map/tnk,nkj->tnj/transpose | solution.py:54
  234.1 6.1 %fusion.43 = bf16[768,4,128]{2,1,0:T(4,128)(2,1)} fusion(f32[768,16,128]{2,1,0:T(8,128)} %copy.64, s32[16]{0:T(128)S(1)} %get-tuple-element.22), kind=kOutput, calls=%fused_computation.61 | convolution fusion | flops 75890752 | bytes 7077952 | tf_op jit(solution)/shard_map/tnj,nf->tfj/dot_general | solution.py:49
  240.2 2.2 copy.92
  242.5 66.9 %all-reduce.3.cloned.1.call-done = (bf16[768,512]{0,1:T(8,128)(2,1)}, bf16[768,512]{0,1:T(8,128)(2,1)}, bf16[768,512]{0,1:T(8,128)(2,1)}) async-done(((bf16[768,512]{0,1:T(8,128)(2,1)}, bf16[768,512]{0,1:T(8,128)(2,1)}, bf16[768,512]{0,1:T(8,128)(2,1)}), (bf16[768,512]{0,1:T(8,128)(2,1)}, bf16[768,512]{0,1:T(8,128)(2,1)}, bf16[768,512]{0,1:T(8,128)(2,1)})) %all-reduce.3.cloned.1.call-update) | async-done | bytes 2359312 | tf_op jit(solution)/shard_map/psum | solution.py:65
  309.4 4.1 fusion.34
  313.5 2.3 copy.66
  315.8 2.3 copy.67
  318.1 3.7 gather_fusion.8
  321.8 3.8 gather_fusion.7
  325.6 3.2 fusion.2
  328.8 3.7 add_bitcast_fusion
  332.5 6.8 %copy.68 = f32[768,16,128]{2,1,0:T(8,128)} copy(f32[768,16,128]{0,2,1:T(8,128)} %add_bitcast_fusion) | data formatting | bytes 12582912 | tf_op jit(solution)/shard_map/add | solution.py:72
  339.3 5.3 convolution_convert_fusion
  346.2 2.3 copy.75
  348.5 2.9 fusion.4
  360.8 4.1 gather_fusion.9
  364.9 2.9 fusion
  371.3 193.6 %reduce-scatter.2.cloned.1.call-done = bf16[24,1024]{1,0:T(8,128)(2,1)} async-done(((bf16[768,1024]{1,0:T(8,128)(2,1)}), bf16[24,1024]{1,0:T(8,128)(2,1)}) %reduce-scatter.2.cloned.1.call-update) | async-done | bytes 49168 | tf_op jit(solution)/shard_map/reduce_scatter | solution.py:75
  (58 shorter events, 31.9 us)
Async XLA Ops:
  7.2 6.3 %copy-start.4 = (bf16[1024,512]{1,0:T(8,128)(2,1)S(1)}, bf16[1024,512]{1,0:T(8,128)(2,1)}, u32[]{:S(2)}) copy-start(bf16[1024,512]{1,0:T(8,128)(2,1)} %param.10) | copy-start | bytes 3145732
  7.2 83.6 %all-gather.5.cloned.1.call-start = ((), (), s32[]{:S(2)}) async-start(), calls=%async_computation.2 | async-start | bytes 1622016 | tf_op jit(solution)/shard_map/all_gather | solution.py:40
  7.9 160.1 %all-gather.3.cloned.1.call-start = ((), (), s32[]{:S(2)}) async-start(), calls=%async_computation.1 | async-start | bytes 1622016 | tf_op jit(solution)/shard_map/all_gather | solution.py:41
  8.7 300.7 %all-reduce.3.cloned.1.call-start = ((), (), s32[]{:S(2)}) async-start(), calls=%async_computation.4 | async-start | bytes 4718592 | tf_op jit(solution)/shard_map/psum | solution.py:65
  15.5 4.6 copy-start.5
  242.4 322.5 %reduce-scatter.2.cloned.1.call-start = ((), (), s32[]{:S(2)}) async-start(), calls=%async_computation.3 | async-start | bytes 1622016 | tf_op jit(solution)/shard_map/reduce_scatter | solution.py:75
  325.6 3.2 copy-start.1
  325.6 3.2 copy-start.3
  351.4 4.2 copy-start.2
  360.8 4.1 copy-start
Sparse Core Ops, SparseCore 0:
  10.6 80.0 all-gather.4
  93.3 74.6 all-gather.2
  242.5 66.7 all-reduce.2
  346.3 218.5 reduce-scatter.1
where the time goes:
time: 581 us; the launch traced here: 572 us
  waiting for transfers between devices  407 us (70%)
  local copies, waits for them, and re-layouts  84.9 us (15%)
  matrix products  59.9 us (10%)
  between operations  14.5 us (2%)
  other arithmetic  5.82 us (1%)
    reduce_scatter x1, waiting for transfers between devices, on_device(): lax.psum_scatter(jnp.einsum('tnk,nd->tdk', slot_dx, onehot_d, precision=h...  194 us
    all_gather x1, waiting for transfers between devices, on_device(): lax.all_gather(grad_out, 'col', axis=0, tiled=True)  74 us
    all_gather x1, waiting for transfers between devices, on_device(): lax.all_gather(tokens, 'col', axis=0, tiled=True)  70.6 us
    psum x1, waiting for transfers between devices, on_device(): lax.psum(dh_part.astype(jnp.bfloat16), 'row').astype(jnp.float32)  66.9 us
    dot_general x3, matrix products, onto_columns(): jnp.einsum('tnj,nf->tfj', slot_vals, onehot_f, precision=high)  18.4 us
  transfers between devices with their start and end apart: 4, of which 4 were waited for; matrix products, arithmetic and copies ran while one was open for 7% of the time, Pallas kernels for 0%

commit v1 on v0

v1 whole, which is shorter than its diff:
```python
import functools

import jax
import jax.numpy as jnp
from jax import lax
from jax.experimental import pallas as pl
from jax.experimental.pallas import tpu as pltpu
from jax.sharding import PartitionSpec as P

MESH = pl.DeviceIdType.MESH
F32 = jnp.float32
BF16 = jnp.bfloat16

NY, NK, NZ, NX = 4, 2, 8, 4
ROWS = 24
TOK = 768
HALF = TOK // 2
DW = 1024
FW = 512
BLK = 128
SLAB = (2 * ROWS, DW // 2)


def nt(a, b):
    return lax.dot_general(a, b, (((1,), (1,)), ((), ())), preferred_element_type=F32)


def nn(a, b):
    return lax.dot_general(a, b, (((1,), (0,)), ((), ())), preferred_element_type=F32)


def kernel(tok_ref, go_ref, wg_hbm, wu_hbm, wd_hbm, flags, order,
           gin_ref, ggate_ref, gup_ref, gdown_ref,
           raw_g, raw_u, raw_d, wgu, wd, gbuf, tbuf, x_all, g_all, dy, xt, perm,
           part, crecv, ssend, yrecv, sown, dgdu, hidt, hid, dxf, rsx, xrecv, zsrc, zrecv,
           wsem, bar_unused, gx_s, gx_r, gz_s, gz_r, tz_s, tz_r, tx_s, tx_r,
           c_s, c_r, y_s, y_r, a_s, a_r, b_s, b_r, rx_s, rx_r, rz_s, rz_r):
    r = lax.axis_index("row")
    c = lax.axis_index("col")
    y, k, z, x = r // 2, lax.rem(r, 2), c // 4, lax.rem(c, 4)

    def at(dy_=0, dk=0, dz=0, dx=0):
        return (lax.rem(y + dy_ + NY, NY) * 2 + lax.rem(k + dk, 2),
                lax.rem(z + dz + NZ, NZ) * 4 + lax.rem(x + dx + NX, NX))

    started = []

    def rc(src, dst, ss, rs, dev):
        return pltpu.make_async_remote_copy(src_ref=src, dst_ref=dst, send_sem=ss, recv_sem=rs,
                                            device_id=dev, device_id_type=MESH)

    def send(src, dst, ss, rs, dev):
        cp = rc(src, dst, ss, rs, dev)
        cp.start()
        started.append(cp)

    loads = [pltpu.make_async_copy(s, d, wsem.at[i])
             for i, (s, d) in enumerate(((wg_hbm, raw_g), (wu_hbm, raw_u), (wd_hbm, raw_d)))]
    for cp in loads:
        cp.start()

    peers = ([dict(dx=d) for d in range(1, NX)] + [dict(dz=d) for d in range(1, NZ)]
             + [dict(dy_=d) for d in range(1, NY)] + [dict(dk=1)])
    bar = pltpu.get_barrier_semaphore()
    for p in peers:
        pl.semaphore_signal(bar, inc=1, device_id=at(**p), device_id_type=MESH)

    def to_slab(v):
        v = v.astype(F32)
        return jnp.concatenate([v[:, :DW // 2], v[:, DW // 2:]], axis=0).astype(BF16)

    gbuf[c] = to_slab(go_ref[...])
    tbuf[c] = to_slab(tok_ref[...])
    pl.semaphore_wait(bar, len(peers))

    def zrel(d):
        return lax.rem(z + d + 2 * NZ, NZ)

    for d in (2, 1, 3):
        send(gbuf.at[c], gbuf.at[c], gx_s.at[d - 1], gx_r.at[d - 1], at(dx=d))

    H = DW // 4

    def tz(direction, s):
        src = zrel(-direction * (s - 1)) * 4 + x
        i = (0 if direction == 1 else 4) + s - 1
        ref = tbuf.at[src]
        if s == 4:
            ref = tbuf.at[src, :, pl.ds(0 if direction == 1 else H, H)]
        return rc(ref, ref, tz_s.at[i], tz_r.at[i], at(dz=direction))

    def gz(direction, s, j):
        src = zrel(-direction * (s - 1)) * 4 + 2 * j
        i = ((0 if direction == 1 else 4) + s - 1) * 2 + j
        ref = gbuf.at[pl.ds(src, 2)]
        return rc(ref, ref, gz_s.at[i], gz_r.at[i], at(dz=direction))

    def tz_wait(direction, s):
        src = zrel(-direction * s) * 4 + x
        i = (0 if direction == 1 else 4) + s - 1
        ref = tbuf.at[src]
        if s == 4:
            ref = tbuf.at[src, :, pl.ds(0 if direction == 1 else H, H)]
        rc(ref, ref, tz_s.at[i], tz_r.at[i], at(dz=direction)).wait_recv()

    def gz_wait(direction, s, j):
        src = zrel(-direction * s) * 4 + 2 * j
        i = ((0 if direction == 1 else 4) + s - 1) * 2 + j
        ref = gbuf.at[pl.ds(src, 2)]
        rc(ref, ref, gz_s.at[i], gz_r.at[i], at(dz=direction)).wait_recv()

    def go(cp):
        cp.start()
        started.append(cp)

    def tx_send(rel):
        idx = zrel(rel) * 4 + x
        for d in (2, 1, 3):
            i = (rel % NZ) * 3 + d - 1
            send(tbuf.at[idx], tbuf.at[idx], tx_s.at[i], tx_r.at[i], at(dx=d))

    go(tz(1, 1))
    go(tz(-1, 1))
    tx_send(0)

    cols = jnp.broadcast_to(order[...], (BLK, TOK)).astype(F32).T
    lane = lax.broadcasted_iota(jnp.int32, (TOK, BLK), 1).astype(F32)
    for j in range(TOK // BLK):
        perm[:, j * BLK:(j + 1) * BLK] = jnp.where(cols == lane + float(j * BLK), 1.0, 0.0).astype(BF16)

    for d in (1, 3, 2):
        idx = z * 4 + lax.rem(x - d + NX, NX)
        rc(gbuf.at[idx], gbuf.at[idx], gx_s.at[d - 1], gx_r.at[d - 1], at(dx=d)).wait_recv()
    for j in range(2):
        go(gz(1, 1, j))
        go(gz(-1, 1, j))

    for s in range(1, 5):
        for direction in (1, -1):
            tz_wait(direction, s)
            if s < 4:
                go(tz(direction, s + 1))
                tx_send(-direction * s)
        if s == 4:
            tx_send(4)
        for j in range(2):
            for direction in (1, -1):
                if s < 4 or (j == 0) == (direction == 1):
                    gz_wait(direction, s, j)
                if s < 3 or (s == 3 and (j == 0) == (direction == 1)):
                    go(gz(direction, s + 1, j))
        if s == 1:
            for cp in loads:
                cp.wait()

            @pl.loop(0, DW // BLK)
            def _(i):
                rows = pl.ds(pl.multiple_of(i * BLK, BLK), BLK)
                for j in range(FW // BLK):
                    f = flags[i, j].astype(F32)
                    cs = slice(j * BLK, (j + 1) * BLK)
                    wgu[j, rows, :BLK] = (raw_g[rows, cs].astype(F32) * f).astype(BF16)
                    wgu[j, rows, BLK:] = (raw_u[rows, cs].astype(F32) * f).astype(BF16)
                    wd[j, :, rows] = (raw_d[cs, rows].astype(F32) * f).astype(BF16)

    for rel in range(NZ):
        for d in (1, 3, 2):
            i = rel * 3 + d - 1
            idx = zrel(rel) * 4 + lax.rem(x - d + NX, NX)
            rc(tbuf.at[idx], tbuf.at[idx], tx_s.at[i], tx_r.at[i], at(dx=d)).wait_recv()

    @pl.loop(0, NZ * NX // 2)
    def _(p):
        rows = pl.ds(pl.multiple_of(p * 2 * ROWS, 2 * ROWS), 2 * ROWS)
        for buf, dst in ((tbuf, x_all), (gbuf, g_all)):
            a = buf[2 * p].astype(F32)
            b = buf[2 * p + 1].astype(F32)
            dst[rows, :DW // 2] = jnp.concatenate([a[:ROWS], b[:ROWS]], axis=0).astype(BF16)
            dst[rows, DW // 2:] = jnp.concatenate([a[ROWS:], b[ROWS:]], axis=0).astype(BF16)

    @pl.loop(0, DW // 256)
    def _(i):
        cs = pl.ds(pl.multiple_of(i * 256, 256), 256)
        dy[:, cs] = nn(perm[...], g_all[:, cs]).astype(BF16)

    def half_rows(h):
        return pl.ds(pl.multiple_of(h * HALF, HALF), HALF)

    def partial(h, yb, slot):
        rows = half_rows(h)
        part[slot, :, :256] = nn(x_all[rows, :], wgu[yb]).astype(BF16)
        part[slot, :, 256:] = nt(dy[rows, :], wd[yb]).astype(BF16)

    def c_copy(d):
        return rc(part.at[d], crecv.at[d], c_s.at[d], c_r.at[d], at(dk=1))

    def ybof(d):
        return lax.rem(y + d, NY)

    @pl.loop(0, NY)
    def _(i):
        d = lax.rem(i + 1, NY)
        partial(1 - k, ybof(d), d)
        c_copy(d).start()

    def y_copy(d):
        return rc(ssend.at[d - 1], yrecv.at[d - 1], y_s.at[d - 1], y_r.at[d - 1], at(dy_=d))

    @pl.loop(1, NY)
    def _(d):
        partial(k, ybof(d), NY)
        c_copy(d).wait_recv()
        ssend[d - 1] = (part[NY].astype(F32) + crecv[d].astype(F32)).astype(BF16)
        y_copy(d).start()

    partial(k, y, NY)

    @pl.loop(0, DW // BLK)
    def _(i):
        cs = pl.ds(pl.multiple_of(i * BLK, BLK), BLK)
        xt[cs, :] = x_all[:, cs].astype(F32).T.astype(BF16)

    c_copy(0).wait_recv()
    for d in (1, 3, 2):
        y_copy(d).wait_recv()

    @pl.loop(0, HALF // 96)
    def _(i):
        rows = pl.ds(pl.multiple_of(i * 96, 96), 96)
        t = part[NY, rows, :].astype(F32) + crecv[0, rows, :].astype(F32)
        for j in range(3):
            t = t + yrecv[j, rows, :].astype(F32)
        gate, up, dh = t[:, :BLK], t[:, BLK:2 * BLK], t[:, 2 * BLK:]
        sig = 1.0 / (1.0 + jnp.exp(-gate))
        silu = gate * sig
        hid[rows, :] = silu * up
        dgdu[k, y, rows, :BLK] = (dh * up * sig * (1.0 + gate * (1.0 - sig))).astype(BF16)
        dgdu[k, y, rows, BLK:] = (dh * silu).astype(BF16)

    hidt[k, y] = hid[...].T.astype(BF16)

    def a_copy(d, which):
        buf = (dgdu, hidt)[which]
        i = (d - 1) * 2 + which
        return rc(buf.at[k, y], buf.at[k, y], a_s.at[i], a_r.at[i], at(dy_=d))

    def a_wait(d, which):
        buf = (dgdu, hidt)[which]
        i = (d - 1) * 2 + which
        src = lax.rem(y - d + NY, NY)
        rc(buf.at[k, src], buf.at[k, src], a_s.at[i], a_r.at[i], at(dy_=d)).wait_recv()

    def b_copy(d, which):
        buf = (dgdu, hidt)[which]
        i = d * 2 + which
        src = lax.rem(y - d + NY, NY)
        return rc(buf.at[k, src], buf.at[k, src], b_s.at[i], b_r.at[i], at(dk=1))

    def b_wait(d, which):
        buf = (dgdu, hidt)[which]
        i = d * 2 + which
        src = lax.rem(y - d + NY, NY)
        rc(buf.at[1 - k, src], buf.at[1 - k, src], b_s.at[i], b_r.at[i], at(dk=1)).wait_recv()

    for which in range(2):
        for d in (2, 1, 3):
            go(a_copy(d, which))
        go(b_copy(0, which))
    for which in range(2):
        for d in (1, 3, 2):
            a_wait(d, which)
            go(b_copy(d, which))
    for which in range(2):
        for d in (0, 1, 3, 2):
            b_wait(d, which)

    for h in range(2):
        @pl.loop(0, DW // 256)
        def _(i, h=h):
            cs = pl.ds(pl.multiple_of(i * 256, 256), 256)
            acc = nt(dgdu[h, 0], wgu[0, cs, :])
            for yb in range(1, NY):
                acc = acc + nt(dgdu[h, yb], wgu[yb, cs, :])
            dxf[h * HALF:(h + 1) * HALF, cs] = acc

    def pack(xx):
        @pl.loop(0, NZ)
        def _(zz):
            v = dxf[pl.ds(pl.multiple_of((zz * 4 + xx) * ROWS, 8), ROWS), :]
            rsx[xx, zz] = jnp.concatenate([v[:, :DW // 2], v[:, DW // 2:]], axis=0).astype(BF16)

    for d in (2, 1, 3):
        xx = lax.rem(x + d, NX)
        pack(xx)
        send(rsx.at[xx], xrecv.at[d - 1], rx_s.at[d - 1], rx_r.at[d - 1], at(dx=d))
    pack(x)

    def weight_grads(first, last):
        @pl.loop(first, last)
        def _(j):
            acc = (nn(xt[:, :HALF], dgdu[0, j]) + nn(xt[:, HALF:], dgdu[1, j]))
            cs = pl.ds(pl.multiple_of(j * BLK, BLK), BLK)
            for i in range(DW // BLK):
                f = flags[i, j].astype(F32)
                blk = acc[i * BLK:(i + 1) * BLK] * f
                ggate_ref[i * BLK:(i + 1) * BLK, cs] = blk[:, :BLK].astype(BF16)
                gup_ref[i * BLK:(i + 1) * BLK, cs] = blk[:, BLK:].astype(BF16)
            acc = nn(hidt[0, j], dy[:HALF, :]) + nn(hidt[1, j], dy[HALF:, :])
            for i in range(DW // BLK):
                f = flags[i, j].astype(F32)
                gdown_ref[cs, i * BLK:(i + 1) * BLK] = (acc[:, i * BLK:(i + 1) * BLK] * f).astype(BF16)

    weight_grads(0, 2)

    for d in (1, 3, 2):
        rc(rsx.at[0], xrecv.at[d - 1], rx_s.at[d - 1], rx_r.at[d - 1], at(dx=d)).wait_recv()

    @pl.loop(0, NZ)
    def _(zz):
        t = rsx[x, zz].astype(F32)
        for j in range(3):
            t = t + xrecv[j, zz].astype(F32)
        zsrc[zz] = t.astype(BF16)

    for d in (4, 3, 5, 2, 6, 1, 7):
        send(zsrc.at[zrel(d)], zrecv.at[d - 1], rz_s.at[d - 1], rz_r.at[d - 1], at(dz=d))

    weight_grads(2, 4)

    for d in (1, 7, 2, 6, 3, 5, 4):
        rc(zsrc.at[0], zrecv.at[d - 1], rz_s.at[d - 1], rz_r.at[d - 1], at(dz=d)).wait_recv()
    t = zsrc[z].astype(F32)
    for j in range(NZ - 1):
        t = t + zrecv[j].astype(F32)
    gin_ref[...] = jnp.concatenate([t[:ROWS], t[ROWS:]], axis=1).astype(BF16)

    for cp in started:
        cp.wait_send()
    for d in range(NY):
        c_copy(d).wait_send()
    for d in range(1, NY):
        y_copy(d).wait_send()


def on_device(tokens, grad_out, w_gate, w_up, w_down, block_flags, token_order):
    vmem = pl.BlockSpec(memory_space=pltpu.VMEM)
    smem = pl.BlockSpec(memory_space=pltpu.SMEM)
    hbm = pl.BlockSpec(memory_space=pl.ANY)
    V = pltpu.VMEM
    sem = lambda n: pltpu.SemaphoreType.DMA((n,))
    n = NZ * NX
    scratch = [
        V((DW, FW), BF16), V((DW, FW), BF16), V((FW, DW), BF16),
        V((NY, DW, 2 * BLK), BF16), V((NY, BLK, DW), BF16),
        V((n,) + SLAB, BF16), V((n,) + SLAB, BF16),
        V((TOK, DW), BF16), V((TOK, DW), BF16), V((TOK, DW), BF16),
        V((DW, TOK), BF16), V((TOK, TOK), BF16),
        V((NY + 1, HALF, 3 * BLK), BF16), V((NY, HALF, 3 * BLK), BF16),
        V((NY - 1, HALF, 3 * BLK), BF16), V((NY - 1, HALF, 3 * BLK), BF16),
        V((8, 128), F32),
        V((NK, NY, HALF, 2 * BLK), BF16), V((NK, NY, BLK, HALF), BF16),
        V((HALF, BLK), F32), V((TOK, DW), F32),
        V((NX, NZ) + SLAB, BF16), V((NX - 1, NZ) + SLAB, BF16),
        V((NZ,) + SLAB, BF16), V((NZ - 1,) + SLAB, BF16),
        sem(3), sem(1), sem(3), sem(3), sem(16), sem(16), sem(8), sem(8), sem(24), sem(24),
        sem(4), sem(4), sem(3), sem(3), sem(6), sem(6), sem(8), sem(8), sem(3), sem(3), sem(7), sem(7),
    ]
    return pl.pallas_call(
        kernel,
        out_shape=(
            jax.ShapeDtypeStruct((ROWS, DW), BF16),
            jax.ShapeDtypeStruct((DW, FW), BF16),
            jax.ShapeDtypeStruct((DW, FW), BF16),
            jax.ShapeDtypeStruct((FW, DW), BF16),
        ),
        in_specs=[vmem, vmem, hbm, hbm, hbm, smem, vmem],
        out_specs=(vmem, vmem, vmem, vmem),
        scratch_shapes=scratch,
        compiler_params=pltpu.CompilerParams(
            collective_id=0, has_side_effects=True, vmem_limit_bytes=58 * 2**20),
        name="layer_backward",
    )(tokens, grad_out, w_gate, w_up, w_down, block_flags, token_order.reshape(1, TOK))


def solution(mesh):
    return jax.shard_map(
        on_device,
        mesh=mesh,
        in_specs=(
            P("col", "row"), P("col", "row"), P("row", "col"), P("row", "col"),
            P("col", "row"), P("row", "col"), P(),
        ),
        out_specs=(P("col", "row"), P("row", "col"), P("row", "col"), P("col", "row")),
        check_vma=False,
    )
```

time: 581 us -> 120 us (0.21)
  the two profiles are of different devices: /device:TPU:8 before, /device:TPU:1 now
where the time goes in v1:
time: 120 us
  Pallas kernels  111 us (92%)
  local copies, waits for them, and re-layouts  8.3 us (7%)
    pallas_call x1, Pallas kernels, on_device(): pl.pallas_call(kernel, out_shape=(jax.ShapeDtypeStruct((ROWS, DW), BF16),...  111 us
    unnamed x11, local copies, waits for them, and re-layouts  7.02 us

profile of v1, /device:TPU:1, one launch (start us, length us, event | category | flops | bytes accessed | tf_op | source)
XLA Modules:
  0.0 120.0 jit_solution(3097995450016322909)
XLA Ops:
  0.6 0.0 copy-start.2
  0.6 1.3 %reshape.11.order = s32[1,768]{1,0:T(1,128)} reshape(s32[768]{0:T(1024)} %param.13) | data formatting | bytes 6144 | tf_op jit(solution)/shard_map/reshape | solution.py:382
  1.9 0.0 copy-done.2
  1.9 0.7 copy.11.flags
  2.6 111.1 %layer_backward.1 = (bf16[24,1024]{1,0:T(8,128)(2,1)}, bf16[1024,512]{1,0:T(8,128)(2,1)}, bf16[1024,512]{1,0:T(8,128)(2,1)}, bf16[512,1024]{1,0:T(8,128)(2,1)}) custom-call(bf16[24,1024]{1,0:T(8,128)(2,1)} %tok_ref.1, bf16[24,1024]{1,0:T(8,128)(2,1)} %go_ref.1, bf16[1024,512]{1,0:T(8,128)(2,1)} %wg_hbm.1, bf16[1024,512]{1,0:T(8,128)(2,1)} %wu_hbm.1, ...), custom_call_target="tpu_custom_call" | custom-call | tf_op jit(solution)/shard_map/layer_backward/pallas_call | solution.py:368
  113.7 1.4 %copy.16 = bf16[24,1024]{1,0:T(8,128)(2,1)} copy(bf16[24,1024]{1,0:T(8,128)(2,1)} %get-tuple-element.8) | data formatting | bytes 98304
  115.1 0.0 copy-start.1
  115.1 2.4 %copy.17 = bf16[1024,512]{1,0:T(8,128)(2,1)} copy(bf16[1024,512]{1,0:T(8,128)(2,1)} %get-tuple-element.9) | data formatting | bytes 2097152
  117.5 0.0 copy-done.1
  117.5 0.0 copy-start
  117.5 1.0 copy.18
  118.4 0.6 copy-done
  119.1 1.0 copy.19
Async XLA Ops:
  0.6 1.3 %copy-start.2 = (s32[8,4]{0,1:T(4,128)S(1)}, s32[8,4]{0,1:T(4,128)}, u32[]{:S(2)}) copy-start(s32[8,4]{0,1:T(4,128)} %param.12) | copy-start | bytes 388
  115.1 2.4 %copy-start.1 = (bf16[1024,512]{1,0:T(8,128)(2,1)S(1)}, bf16[1024,512]{1,0:T(8,128)(2,1)}, u32[]{:S(2)}) copy-start(bf16[1024,512]{1,0:T(8,128)(2,1)} %get-tuple-element.10) | copy-start | bytes 3145732
  117.5 1.6 %copy-start = (bf16[512,1024]{1,0:T(8,128)(2,1)S(1)}, bf16[512,1024]{1,0:T(8,128)(2,1)}, u32[]{:S(2)}) copy-start(bf16[512,1024]{1,0:T(8,128)(2,1)} %get-tuple-element.11) | copy-start | bytes 3145732

commit v2 on v0

v2 whole, which is shorter than its diff:
```python
import functools

import jax
import jax.numpy as jnp
from jax import lax
from jax.experimental import pallas as pl
from jax.experimental.pallas import tpu as pltpu
from jax.sharding import PartitionSpec as P

MESH = pl.DeviceIdType.MESH
F32 = jnp.float32
BF16 = jnp.bfloat16

NY, NK, NZ, NX = 4, 2, 8, 4
ROWS = 24
TOK = 768
HALF = TOK // 2
DW = 1024
FW = 512
BLK = 128
SLAB = (2 * ROWS, DW // 2)
PLANE = NX * ROWS
RHO = ((0, -1), (1, -2), (2, -3), (3, 4))
NQ = len(RHO)
NP = 4
SW = NX // NP


def nt(a, b):
    return lax.dot_general(a, b, (((1,), (1,)), ((), ())), preferred_element_type=F32)


def nn(a, b):
    return lax.dot_general(a, b, (((1,), (0,)), ((), ())), preferred_element_type=F32)


def kernel(tok_hbm, go_hbm, wg_hbm, wu_hbm, wd_hbm, flags, order,
           gin_hbm, ggate_hbm, gup_hbm, gdown_hbm,
           tok_ref, go_ref, gin_ref, ggate_ref, gup_ref, gdown_ref,
           raw_g, raw_u, raw_d, wgu, wd, ga, gb, ta, tb, x_all, g_all, dy, xt, perm, ocol,
           part, crecv, ssend, yrecv, dhu, dhp, dhc, dhs, dhy, dht, act, hidt, dxf, rsx, xrecv, zsrc, zrecv,
           wsem, osem, gxa_s, gxa_r, gza_s, gza_r, gzb_s, gzb_r, gxb_s, gxb_r,
           txa_s, txa_r, tza_s, tza_r, tzb_s, tzb_r, txb_s, txb_r,
           c_s, c_r, y_s, y_r, h_s, h_r, a_s, a_r, b_s, b_r, rx_s, rx_r, rz_s, rz_r):
    r = lax.axis_index("row")
    c = lax.axis_index("col")
    y, k, z, x = r // 2, lax.rem(r, 2), c // 4, lax.rem(c, 4)

    def at(dy_=0, dk=0, dz=0, dx=0):
        return (lax.rem(y + dy_ + NY, NY) * 2 + lax.rem(k + dk, 2),
                lax.rem(z + dz + NZ, NZ) * 4 + lax.rem(x + dx + NX, NX))

    def zrel(d):
        return lax.rem(z + d + 2 * NZ, NZ)

    def yrel(d):
        return lax.rem(y + d + NY, NY)

    def xrel(d):
        return lax.rem(x + d + NX, NX)

    started = []

    def rc(src, dst, ss, rs, dev):
        return pltpu.make_async_remote_copy(src_ref=src, dst_ref=dst, send_sem=ss, recv_sem=rs,
                                            device_id=dev, device_id_type=MESH)

    def go(cp):
        cp.start()
        started.append(cp)


    peers = ([dict(dx=d) for d in range(1, NX)] + [dict(dz=d) for d in (1, 7, 2, 6, 3, 5, 4)]
             + [dict(dy_=d) for d in range(1, NY)] + [dict(dk=1)])
    bar = pltpu.get_barrier_semaphore()
    for p in peers:
        pl.semaphore_signal(bar, inc=1, device_id=at(**p), device_id_type=MESH)

    loads = [pltpu.make_async_copy(s, d, wsem.at[i])
             for i, (s, d) in enumerate(((go_hbm, go_ref), (tok_hbm, tok_ref),
                                         (wd_hbm, raw_d), (wg_hbm, raw_g), (wu_hbm, raw_u)))]
    for cp in loads:
        cp.start()
    stores = []

    def store(src, dst):
        cp = pltpu.make_async_copy(src, dst, osem.at[len(stores)])
        cp.start()
        stores.append(cp)

    QW = DW // 4

    def to_slabs(ref, a, b):
        v = ref[...].astype(F32)
        a[c] = jnp.concatenate([v[:, :QW], v[:, QW:2 * QW]], axis=0).astype(BF16)
        b[c] = jnp.concatenate([v[:, 2 * QW:3 * QW], v[:, 3 * QW:]], axis=0).astype(BF16)

    loads[0].wait()
    to_slabs(go_ref, ga, gb)
    loads[1].wait()
    to_slabs(tok_ref, ta, tb)
    pl.semaphore_wait(bar, len(peers))

    class Gather:
        def __init__(self, a, b, xa_s, xa_r, za_s, za_r, zb_s, zb_r, xb_s, xb_r):
            self.a, self.b = a, b
            self.xa, self.za, self.zb, self.xb = (xa_s, xa_r), (za_s, za_r), (zb_s, zb_r), (xb_s, xb_r)

        def xa_copy(self, d, src):
            ref = self.a.at[src]
            return rc(ref, ref, self.xa[0].at[d - 1], self.xa[1].at[d - 1], at(dx=d))

        def za_copy(self, direction, s, j, src_rel):
            i = ((0 if direction == 1 else 4) + s - 1) * NP + j
            ref = self.a.at[pl.ds(zrel(src_rel) * NX + j * SW, SW)]
            return rc(ref, ref, self.za[0].at[i], self.za[1].at[i], at(dz=direction))

        def zb_copy(self, direction, s, src_rel):
            i = (0 if direction == 1 else 4) + s - 1
            src = zrel(src_rel) * NX + x
            ref = self.b.at[src]
            if s == 4:
                ref = self.b.at[src, :, pl.ds(0 if direction == 1 else QW // 2, QW // 2)]
            return rc(ref, ref, self.zb[0].at[i], self.zb[1].at[i], at(dz=direction))

        def xb_copy(self, rel, d, src):
            i = (rel % NZ) * 3 + d - 1
            ref = self.b.at[src]
            return rc(ref, ref, self.xb[0].at[i], self.xb[1].at[i], at(dx=d))

        def xb_send(self, rel):
            for d in (2, 1, 3):
                go(self.xb_copy(rel, d, zrel(rel) * NX + x))

        def xb_wait(self, rel):
            for d in (1, 3, 2):
                self.xb_copy(rel, d, zrel(rel) * NX + xrel(-d)).wait_recv()

        def start(self):
            for d in (2, 1, 3):
                go(self.xa_copy(d, c))
            go(self.zb_copy(1, 1, 0))
            go(self.zb_copy(-1, 1, 0))
            self.xb_send(0)

        def step(self, t):
            if t <= 4:
                for direction in (1, -1):
                    self.zb_copy(direction, t, -direction * t).wait_recv()
                    if t < 4:
                        go(self.zb_copy(direction, t + 1, -direction * t))
                        self.xb_send(-direction * t)
                if t == 4:
                    self.xb_send(4)
            if t == 1:
                for d in (1, 3, 2):
                    self.xa_copy(d, z * NX + xrel(-d)).wait_recv()
                for j in range(NP):
                    for direction in (1, -1):
                        go(self.za_copy(direction, 1, j, 0))
                return
            s = t - 1
            for j in range(NP):
                for direction in (1, -1):
                    mine = (j < NP // 2) == (direction == 1)
                    if s < 4 or mine:
                        self.za_copy(direction, s, j, -direction * s).wait_recv()
                    if s < 3 or (s == 3 and mine):
                        go(self.za_copy(direction, s + 1, j, -direction * s))

    G = Gather(ga, gb, gxa_s, gxa_r, gza_s, gza_r, gzb_s, gzb_r, gxb_s, gxb_r)
    T = Gather(ta, tb, txa_s, txa_r, tza_s, tza_r, tzb_s, tzb_r, txb_s, txb_r)

    def masks(i0, i1):
        @pl.loop(i0, i1)
        def _(i):
            rows = pl.ds(pl.multiple_of(i * BLK, BLK), BLK)
            for j in range(FW // BLK):
                f = flags[j, i].astype(F32)
                cs = slice(j * BLK, (j + 1) * BLK)
                wgu[j, rows, :BLK] = (raw_g[rows, cs].astype(F32) * f).astype(BF16)
                wgu[j, rows, BLK:] = (raw_u[rows, cs].astype(F32) * f).astype(BF16)
                wd[cs, rows] = (raw_d[cs, rows].astype(F32) * f).astype(BF16)

    def unslab(a, b, c0, dst, row0):
        rows = pl.ds(row0, 2 * ROWS)
        for n, buf in enumerate((a, b)):
            v, w = buf[c0].astype(F32), buf[c0 + 1].astype(F32)
            dst[rows, 2 * n * QW:(2 * n + 1) * QW] = jnp.concatenate([v[:ROWS], w[:ROWS]], axis=0).astype(BF16)
            dst[rows, (2 * n + 1) * QW:(2 * n + 2) * QW] = jnp.concatenate([v[ROWS:], w[ROWS:]], axis=0).astype(BF16)

    def rows_of(q, p):
        return slice(p * HALF + q * PLANE, p * HALF + (q + 1) * PLANE)

    def krows(q):
        return pl.ds(pl.multiple_of(k * HALF + q * PLANE, 32), PLANE)

    kplane = pl.ds(pl.multiple_of(k * PLANE, 32), PLANE)
    khalf = pl.ds(pl.multiple_of(k * HALF, HALF), HALF)

    def c_copy(q):
        sib = pl.ds(pl.multiple_of((1 - k) * PLANE, 32), PLANE)
        return rc(part.at[q, :, sib], crecv.at[q], c_s.at[q], c_r.at[q], at(dk=1))

    def stage_p(q):
        for p in range(2):
            plane = zrel(RHO[q][p])
            T.xb_wait(RHO[q][p])
            for xx in (0, 2):
                unslab(ta, tb, plane * NX + xx, x_all, p * HALF + q * PLANE + xx * ROWS)
        lhs = jnp.concatenate([x_all[rows_of(q, 0), :], x_all[rows_of(q, 1), :]], axis=0)

        @pl.loop(0, NY)
        def _(d):
            part[q, d] = nn(lhs, wgu[yrel(d)]).astype(BF16)

        go(c_copy(q))

    def y_copy(q, d):
        i = q * 3 + d - 1
        return rc(ssend.at[q, d - 1], yrecv.at[q, d - 1], y_s.at[i], y_r.at[i], at(dy_=d))

    def stage_c(q):
        c_copy(q).wait_recv()
        for d in (2, 1, 3):
            ssend[q, d - 1] = (part[q, d, kplane, :].astype(F32) + crecv[q, d].astype(F32)).astype(BF16)
            go(y_copy(q, d))

    def a_copy(q, d, src):
        i = q * 3 + d - 1
        ref = act.at[src, krows(q)]
        return rc(ref, ref, a_s.at[i], a_r.at[i], at(dy_=d))

    def b_copy(q, d, src, half):
        i = q * 4 + d
        ref = act.at[src, pl.ds(pl.multiple_of(half * HALF + q * PLANE, 32), PLANE)]
        return rc(ref, ref, b_s.at[i], b_r.at[i], at(dk=1))

    def stage_y(q):
        for d in (1, 3, 2):
            y_copy(q, d).wait_recv()
        t = part[q, 0, kplane, :].astype(F32) + crecv[q, 0].astype(F32)
        for j in range(3):
            t = t + yrecv[q, j].astype(F32)
        gate, up = t[:, :BLK], t[:, BLK:]
        dh = dht[q * PLANE:(q + 1) * PLANE, :]
        sig = 1.0 / (1.0 + jnp.exp(-gate))
        silu = gate * sig
        rows = krows(q)
        act[y, rows, :BLK] = (dh * up * sig * (1.0 + gate * (1.0 - sig))).astype(BF16)
        act[y, rows, BLK:2 * BLK] = (dh * silu).astype(BF16)
        act[y, rows, 2 * BLK:] = (silu * up).astype(BF16)
        for d in (2, 1, 3):
            go(a_copy(q, d, y))
        go(b_copy(q, 0, y, k))

    def stage_a(q):
        for d in (1, 3, 2):
            a_copy(q, d, yrel(-d)).wait_recv()
            go(b_copy(q, d, yrel(-d), k))

    def rx_copy(q, d):
        i = q * 3 + d - 1
        return rc(rsx.at[q, xrel(d)], xrecv.at[q, d - 1], rx_s.at[i], rx_r.at[i], at(dx=d))

    def stage_b(q):
        for d in (0, 1, 3, 2):
            b_copy(q, d, yrel(-d), 1 - k).wait_recv()

        @pl.loop(0, DW // 256)
        def _(i):
            cs = pl.ds(pl.multiple_of(i * 256, 256), 256)
            acc = None
            for yb in range(NY):
                lhs = jnp.concatenate([act[yb, rows_of(q, 0), :2 * BLK], act[yb, rows_of(q, 1), :2 * BLK]], axis=0)
                t = nt(lhs, wgu[yb, cs, :])
                acc = t if acc is None else acc + t
            dxf[q % 2, :, cs] = acc

        for p in range(2):
            for xx in range(NX):
                v = dxf[q % 2, p * PLANE + xx * ROWS:p * PLANE + (xx + 1) * ROWS, :]
                rsx[q, xx, p] = jnp.concatenate([v[:, :DW // 2], v[:, DW // 2:]], axis=0).astype(BF16)
        for d in (2, 1, 3):
            go(rx_copy(q, d))

    def rz_copy(rho, src):
        i = rho % NZ - 1
        return rc(src, zrecv.at[i], rz_s.at[i], rz_r.at[i], at(dz=rho))

    def stage_x(q):
        for d in (1, 3, 2):
            rx_copy(q, d).wait_recv()
        for p in range(2):
            t = rsx[q, x, p].astype(F32)
            for j in range(3):
                t = t + xrecv[q, j, p].astype(F32)
            zsrc[q, p] = t.astype(BF16)
            if RHO[q][p] != 0:
                go(rz_copy(RHO[q][p], zsrc.at[q, p]))

    def h_copy(d):
        if d == 0:
            sib = pl.ds(pl.multiple_of((1 - k) * HALF, HALF), HALF)
            return rc(dhp.at[:, sib], dhc, h_s.at[0], h_r.at[0], at(dk=1))
        return rc(dhs.at[d - 1], dhy.at[d - 1], h_s.at[d], h_r.at[d], at(dy_=d))

    def gpair(q):
        parts = []
        for p in range(2):
            plane = zrel(RHO[q][p])
            G.xb_wait(RHO[q][p])
            for xx in (0, 2):
                unslab(ga, gb, plane * NX + xx, g_all, pl.multiple_of(plane * PLANE + xx * ROWS, 2 * ROWS))
            parts.append(pl.ds(pl.multiple_of(plane * PLANE, 32), PLANE))
        lhs = jnp.concatenate([g_all[parts[0], :], g_all[parts[1], :]], axis=0)
        for i in range(2):
            t = nt(lhs, wd[i * 256:(i + 1) * 256, :]).astype(BF16)
            dhu[parts[0], i * 256:(i + 1) * 256] = t[:PLANE]
            dhu[parts[1], i * 256:(i + 1) * 256] = t[PLANE:]

    def permute():
        @pl.loop(0, DW // 256)
        def _(i):
            cs = pl.ds(pl.multiple_of(i * 256, 256), 256)
            dy[:, cs] = nn(perm[...], g_all[:, cs]).astype(BF16)

    def dh_partial():
        for i in range(2):
            t = nn(perm[...], dhu[:, i * 256:(i + 1) * 256])
            dhp[2 * i] = t[:, :BLK].astype(BF16)
            dhp[2 * i + 1] = t[:, BLK:].astype(BF16)
        go(h_copy(0))

    def dh_pair():
        h_copy(0).wait_recv()
        for d in (2, 1, 3):
            yb = yrel(d)
            dhs[d - 1] = (dhp[yb, khalf, :].astype(F32) + dhc[yb].astype(F32)).astype(BF16)
            go(h_copy(d))

    def dh_total():
        for d in (1, 3, 2):
            h_copy(d).wait_recv()
        t = dhp[y, khalf, :].astype(F32) + dhc[y].astype(F32)
        for j in range(3):
            t = t + dhy[j].astype(F32)
        dht[...] = t

    def transpose_tokens():
        @pl.loop(0, DW // BLK)
        def _(i):
            cs = pl.ds(pl.multiple_of(i * BLK, BLK), BLK)
            xt[cs, :] = x_all[:, cs].astype(F32).T.astype(BF16)

    def weight_grads(first, last):
        weight_grads_of(first, last)
        cs = slice(first * BLK, last * BLK)
        store(ggate_ref.at[:, cs], ggate_hbm.at[:, cs])
        store(gup_ref.at[:, cs], gup_hbm.at[:, cs])
        store(gdown_ref.at[cs], gdown_hbm.at[cs])

    def weight_grads_of(first, last):
        @pl.loop(first, last)
        def _(j):
            acc = nn(xt[...], act[j, :, :2 * BLK])
            cs = pl.ds(pl.multiple_of(j * BLK, BLK), BLK)
            for i in range(DW // BLK):
                f = flags[j, i].astype(F32)
                blk = acc[i * BLK:(i + 1) * BLK] * f
                ggate_ref[i * BLK:(i + 1) * BLK, cs] = blk[:, :BLK].astype(BF16)
                gup_ref[i * BLK:(i + 1) * BLK, cs] = blk[:, BLK:].astype(BF16)
            hidt[...] = act[j, :, 2 * BLK:].astype(F32).T.astype(BF16)
            acc = nn(hidt[...], dy[...])
            for i in range(DW // BLK):
                f = flags[j, i].astype(F32)
                gdown_ref[cs, i * BLK:(i + 1) * BLK] = (acc[:, i * BLK:(i + 1) * BLK] * f).astype(BF16)

    def make_perm():
        ocol[...] = jnp.broadcast_to(order[...].reshape(1, TOK), (BLK, TOK)).astype(F32).T
        lane = lax.broadcasted_iota(jnp.int32, (PLANE, BLK), 1).astype(F32)
        for q in range(NQ):
            for p in range(2):
                o = ocol[pl.ds(pl.multiple_of(zrel(RHO[q][p]) * PLANE, 32), PLANE), :]
                for j in range(TOK // BLK):
                    perm[rows_of(q, p), j * BLK:(j + 1) * BLK] = jnp.where(o == lane + float(j * BLK), 1.0, 0.0).astype(BF16)

    T.start()
    G.start()
    make_perm()
    T.step(1)
    G.step(1)
    for cp in loads[2:]:
        cp.wait()
    masks(0, 4)
    T.step(2)
    G.step(2)
    masks(4, 8)
    T.step(3)
    G.step(3)
    stage_p(0)
    gpair(0)
    T.step(4)
    G.step(4)
    stage_p(1)
    gpair(1)
    T.step(5)
    stage_c(0)
    stage_p(2)
    G.step(5)
    gpair(2)
    gpair(3)
    dh_partial()
    stage_c(1)
    stage_p(3)
    stage_c(2)
    dh_pair()
    stage_c(3)
    dh_total()
    stage_y(3)
    stage_y(2)
    stage_y(1)
    stage_a(3)
    stage_y(0)
    stage_a(2)
    stage_b(3)
    stage_a(1)
    stage_b(2)
    stage_a(0)
    stage_x(3)
    stage_b(1)
    stage_x(2)
    stage_b(0)
    permute()
    transpose_tokens()
    weight_grads(0, 1)
    stage_x(1)
    weight_grads(1, 2)
    stage_x(0)
    weight_grads(2, 4)
    for d in (1, 7, 2, 6, 3, 5, 4):
        rz_copy(d, zsrc.at[0, 0]).wait_recv()
    t = zsrc[0, 0].astype(F32)
    for j in range(NZ - 1):
        t = t + zrecv[j].astype(F32)
    gin_ref[...] = jnp.concatenate([t[:ROWS], t[ROWS:]], axis=1).astype(BF16)

    store(gin_ref, gin_hbm)
    for cp in started:
        cp.wait_send()
    for cp in stores:
        cp.wait()


def copy_kernel(a, b, c, d, oa, ob, oc, od, va, vb, vc, vd, lsem, ssem):
    loads, stores = [], []
    for src, mid, dst, n in ((b, vb, ob, 4), (c, vc, oc, 4), (d, vd, od, 4), (a, va, oa, 1)):
        step = src.shape[0] // n
        for i in range(n):
            rows = pl.ds(i * step, step)
            loads.append(pltpu.make_async_copy(src.at[rows], mid.at[rows], lsem.at[len(loads)]))
            stores.append(pltpu.make_async_copy(mid.at[rows], dst.at[rows], ssem.at[len(stores)]))
    for cp in loads:
        cp.start()
    for ld, st in zip(loads, stores):
        ld.wait()
        st.start()
    for cp in stores:
        cp.wait()


def on_device(tokens, grad_out, w_gate, w_up, w_down, block_flags, token_order):
    vmem = pl.BlockSpec(memory_space=pltpu.VMEM)
    smem = pl.BlockSpec(memory_space=pltpu.SMEM)
    hbm = pl.BlockSpec(memory_space=pl.ANY)
    V = pltpu.VMEM
    n = NZ * NX
    half_slab = (n, 2 * ROWS, DW // 4)
    sems = [5, 10]
    for _ in range(2):
        for m in (3, 8 * NP, 8, 24):
            sems += [m, m]
    for m in (NQ, 3 * NQ, 4, 3 * NQ, 4 * NQ, 3 * NQ, 7):
        sems += [m, m]
    scratch = [
        V((ROWS, DW), BF16), V((ROWS, DW), BF16), V((ROWS, DW), BF16),
        V((DW, FW), BF16), V((DW, FW), BF16), V((FW, DW), BF16),
        V((DW, FW), BF16), V((DW, FW), BF16), V((FW, DW), BF16),
        V((NY, DW, 2 * BLK), BF16), V((FW, DW), BF16),
        V(half_slab, BF16), V(half_slab, BF16), V(half_slab, BF16), V(half_slab, BF16),
        V((TOK, DW), BF16), V((TOK, DW), BF16), V((TOK, DW), BF16),
        V((DW, TOK), BF16), V((TOK, TOK), BF16), V((TOK, BLK), F32),
        V((NQ, NY, 2 * PLANE, 2 * BLK), BF16), V((NQ, NY, PLANE, 2 * BLK), BF16),
        V((NQ, NY - 1, PLANE, 2 * BLK), BF16), V((NQ, NY - 1, PLANE, 2 * BLK), BF16),
        V((TOK, FW), BF16), V((NY, TOK, BLK), BF16), V((NY, HALF, BLK), BF16),
        V((NY - 1, HALF, BLK), BF16), V((NY - 1, HALF, BLK), BF16), V((HALF, BLK), F32),
        V((NY, TOK, 3 * BLK), BF16), V((BLK, TOK), BF16),
        V((2, 2 * PLANE, DW), F32),
        V((NQ, NX, 2) + SLAB, BF16), V((NQ, NX - 1, 2) + SLAB, BF16),
        V((NQ, 2) + SLAB, BF16), V((NZ - 1,) + SLAB, BF16),
    ] + [pltpu.SemaphoreType.DMA((m,)) for m in sems]
    out_shape = (
        jax.ShapeDtypeStruct((ROWS, DW), BF16),
        jax.ShapeDtypeStruct((DW, FW), BF16),
        jax.ShapeDtypeStruct((DW, FW), BF16),
        jax.ShapeDtypeStruct((FW, DW), BF16),
    )
    out = pl.pallas_call(
        kernel,
        out_shape=out_shape,
        in_specs=[hbm, hbm, hbm, hbm, hbm, smem, vmem],
        out_specs=(hbm,) * 4,
        scratch_shapes=scratch,
        compiler_params=pltpu.CompilerParams(
            collective_id=0, has_side_effects=True, vmem_limit_bytes=58 * 2**20),
        name="layer_backward",
    )(tokens, grad_out, w_gate, w_up, w_down, block_flags.T, token_order)
    return pl.pallas_call(
        copy_kernel,
        out_shape=out_shape,
        in_specs=[hbm] * 4,
        out_specs=(hbm,) * 4,
        scratch_shapes=[V(o.shape, o.dtype) for o in out_shape] + [pltpu.SemaphoreType.DMA((13,))] * 2,
        compiler_params=pltpu.CompilerParams(vmem_limit_bytes=58 * 2**20),
        name="hand_over",
    )(*out)


def solution(mesh):
    return jax.shard_map(
        on_device,
        mesh=mesh,
        in_specs=(
            P("col", "row"), P("col", "row"), P("row", "col"), P("row", "col"),
            P("col", "row"), P("row", "col"), P(),
        ),
        out_specs=(P("col", "row"), P("row", "col"), P("row", "col"), P("col", "row")),
        check_vma=False,
    )
```

time: 581 us -> 87 us (0.15); the launches traced: 572 us -> 86.9 us
  waiting for transfers between devices: 407 us -> 0 us
  Pallas kernels: 0 us -> 86.3 us
  local copies, waits for them, and re-layouts: 84.9 us -> 0 us
  matrix products: 59.9 us -> 0 us
  between operations: 14.5 us -> 0.64 us
  other arithmetic: 5.82 us -> 0 us
    reduce_scatter x1 -> x0, waiting for transfers between devices: 194 us -> none  [on_device(): lax.psum_scatter(jnp.einsum('tnk,nd->tdk', slot_dx, onehot_d, precision=h...]
    all_gather x2 -> x0, waiting for transfers between devices: 145 us -> none  [the longest x1 74 us: on_device(): lax.all_gather(grad_out, 'col', axis=0, tiled=True)]
    pallas_call x0 -> x2, Pallas kernels: none -> 86.3 us  [the longest x1 83.4 us: on_device(): pl.pallas_call(kernel, out_shape=out_shape, in_specs=[hbm, hbm, hbm, hbm,...]
    psum x1 -> x0, waiting for transfers between devices: 66.9 us -> none  [on_device(): lax.psum(dh_part.astype(jnp.bfloat16), 'row').astype(jnp.float32)]
    dot_general x15 -> x0, matrix products: 59.9 us -> none  [the longest x3 18.4 us: onto_columns(): jnp.einsum('tnj,nf->tfj', slot_vals, onehot_f, precision=high)]
    gather x10 -> x0, local copies, waits for them, and re-layouts: 28.5 us -> none  [the longest x1 5.43 us: on_device(): dy_all = dy_all[token_order]]
    transpose x3 -> x0, local copies, waits for them, and re-layouts: 19.9 us -> none  [the longest x1 6.74 us: on_device(): jnp.einsum('tnk,nkj->tnj', x_packed, up_blocks, preferred_element_type=jn...]
    reshape x11 -> x0, local copies, waits for them, and re-layouts: 12.4 us -> none  [the longest x1 2.33 us: on_device(): hidden_p = hidden.reshape(total, nbf, blk)[:, col_block, :]]
  transfers between devices with their start and end apart: 4 -> 0, of which waited for: 4 -> 0; matrix products, arithmetic and copies ran while one was open for 7% -> 0% of each run, Pallas kernels for 0% -> 0%
where the time goes in v2:
time: 87 us; the launch traced here: 86.9 us
  Pallas kernels  86.3 us (99%)
    pallas_call x1, Pallas kernels, on_device(): pl.pallas_call(kernel, out_shape=out_shape, in_specs=[hbm, hbm, hbm, hbm,...  83.4 us
    pallas_call x1, Pallas kernels, on_device(): pl.pallas_call(copy_kernel, out_shape=out_shape, in_specs=[hbm] * 4, out_...  2.83 us

profile of v2, /device:TPU:8, one launch (start us, length us, event | category | flops | bytes accessed | tf_op | source)
XLA Modules:
  0.0 86.9 jit_solution(2939293668701826339)
XLA Ops:
  0.6 83.4 %layer_backward.1 = (bf16[24,1024]{1,0:T(8,128)(2,1)}, bf16[1024,512]{1,0:T(8,128)(2,1)}, bf16[1024,512]{1,0:T(8,128)(2,1)}, bf16[512,1024]{1,0:T(8,128)(2,1)}) custom-call(bf16[24,1024]{1,0:T(8,128)(2,1)} %tok_hbm.1, bf16[24,1024]{1,0:T(8,128)(2,1)} %go_hbm.1, bf16[1024,512]{1,0:T(8,128)(2,1)} %wg_hbm.1, bf16[1024,512]{1,0:T(8,128)(2,1)} %wu_hbm.1, ...), custom_call_target="tpu_custom_call" | custom-call | tf_op jit(solution)/shard_map/layer_backward/pallas_call | solution.py:508
  84.1 2.8 %hand_over.1 = (bf16[24,1024]{1,0:T(8,128)(2,1)}, bf16[1024,512]{1,0:T(8,128)(2,1)}, bf16[1024,512]{1,0:T(8,128)(2,1)}, bf16[512,1024]{1,0:T(8,128)(2,1)}) custom-call(bf16[24,1024]{1,0:T(8,128)(2,1)} %get-tuple-element.8.a, bf16[1024,512]{1,0:T(8,128)(2,1)} %get-tuple-element.9.b, bf16[1024,512]{1,0:T(8,128)(2,1)} %get-tuple-element.10.c, ...), custom_call_target="tpu_custom_call" | custom-call | tf_op jit(solution)/shard_map/hand_over/pallas_call | solution.py:518

commit v3 on v2

--- a/solution.py
+++ b/solution.py
@@ -37,11 +37,11 @@
 def kernel(tok_hbm, go_hbm, wg_hbm, wu_hbm, wd_hbm, flags, order,
            gin_hbm, ggate_hbm, gup_hbm, gdown_hbm,
            tok_ref, go_ref, gin_ref, ggate_ref, gup_ref, gdown_ref,
-           raw_g, raw_u, raw_d, wgu, wd, ga, gb, ta, tb, x_all, g_all, dy, xt, perm, ocol,
-           part, crecv, ssend, yrecv, dhu, dhp, dhc, dhs, dhy, dht, act, hidt, dxf, rsx, xrecv, zsrc, zrecv,
+           raw_g, raw_u, raw_d, wgu, wgut, wd, ga, gb, ta, tb, x_all, g_all, dy, xt, perm, ocol,
+           part, crecv, ssend, yrecv, dhu, dhp, dhc, dhs, dhy, dht, act, hid, hidt, dxf, rsx, xrecv, zsrc, zrecv,
            wsem, osem, gxa_s, gxa_r, gza_s, gza_r, gzb_s, gzb_r, gxb_s, gxb_r,
            txa_s, txa_r, tza_s, tza_r, tzb_s, tzb_r, txb_s, txb_r,
-           c_s, c_r, y_s, y_r, h_s, h_r, a_s, a_r, b_s, b_r, rx_s, rx_r, rz_s, rz_r):
+           c_s, c_r, y_s, y_r, h_s, h_r, a_s, a_r, b_s, b_r, rx_s, rx_r, rz_s, rz_r, e_s, e_r, f_s, f_r):
     r = lax.axis_index("row")
     c = lax.axis_index("col")
     y, k, z, x = r // 2, lax.rem(r, 2), c // 4, lax.rem(c, 4)
@@ -143,13 +143,20 @@
             go(self.zb_copy(-1, 1, 0))
             self.xb_send(0)
 
-        def step(self, t):
+        def step(self, t, fill=()):
+            fill = list(fill)
+
+            def work():
+                if fill:
+                    fill.pop(0)()
+
             if t <= 4:
                 for direction in (1, -1):
                     self.zb_copy(direction, t, -direction * t).wait_recv()
                     if t < 4:
                         go(self.zb_copy(direction, t + 1, -direction * t))
                         self.xb_send(-direction * t)
+                    work()
                 if t == 4:
                     self.xb_send(4)
             if t == 1:
@@ -158,6 +165,8 @@
                 for j in range(NP):
                     for direction in (1, -1):
                         go(self.za_copy(direction, 1, j, 0))
+                while fill:
+                    work()
                 return
             s = t - 1
             for j in range(NP):
@@ -167,6 +176,9 @@
                         self.za_copy(direction, s, j, -direction * s).wait_recv()
                     if s < 3 or (s == 3 and mine):
                         go(self.za_copy(direction, s + 1, j, -direction * s))
+                work()
+            while fill:
+                work()
 
     G = Gather(ga, gb, gxa_s, gxa_r, gza_s, gza_r, gzb_s, gzb_r, gxb_s, gxb_r)
     T = Gather(ta, tb, txa_s, txa_r, tza_s, tza_r, tzb_s, tzb_r, txb_s, txb_r)
@@ -202,19 +214,25 @@
         sib = pl.ds(pl.multiple_of((1 - k) * PLANE, 32), PLANE)
         return rc(part.at[q, :, sib], crecv.at[q], c_s.at[q], c_r.at[q], at(dk=1))
 
-    def stage_p(q):
-        for p in range(2):
+    def pieces_p(q):
+        def rows(p):
             plane = zrel(RHO[q][p])
             T.xb_wait(RHO[q][p])
             for xx in (0, 2):
                 unslab(ta, tb, plane * NX + xx, x_all, p * HALF + q * PLANE + xx * ROWS)
-        lhs = jnp.concatenate([x_all[rows_of(q, 0), :], x_all[rows_of(q, 1), :]], axis=0)
-
-        @pl.loop(0, NY)
-        def _(d):
+
+        def product(d):
+            lhs = jnp.concatenate([x_all[rows_of(q, 0), :], x_all[rows_of(q, 1), :]], axis=0)
             part[q, d] = nn(lhs, wgu[yrel(d)]).astype(BF16)
-
-        go(c_copy(q))
+            if d == NY - 1:
+                go(c_copy(q))
+
+        return ([functools.partial(rows, p) for p in range(2)]
+                + [functools.partial(product, d) for d in range(NY)])
+
+    def stage_p(q):
+        for piece in pieces_p(q):
+            piece()
 
     def y_copy(q, d):
         i = q * 3 + d - 1
@@ -228,12 +246,12 @@
 
     def a_copy(q, d, src):
         i = q * 3 + d - 1
-        ref = act.at[src, krows(q)]
+        ref = act.at[krows(q), pl.ds(pl.multiple_of(src * 256, 256), 256)]
         return rc(ref, ref, a_s.at[i], a_r.at[i], at(dy_=d))
 
     def b_copy(q, d, src, half):
         i = q * 4 + d
-        ref = act.at[src, pl.ds(pl.multiple_of(half * HALF + q * PLANE, 32), PLANE)]
+        ref = act.at[pl.ds(pl.multiple_of(half * HALF + q * PLANE, 32), PLANE), pl.ds(pl.multiple_of(src * 256, 256), 256)]
         return rc(ref, ref, b_s.at[i], b_r.at[i], at(dk=1))
 
     def stage_y(q):
@@ -247,12 +265,34 @@
         sig = 1.0 / (1.0 + jnp.exp(-gate))
         silu = gate * sig
         rows = krows(q)
-        act[y, rows, :BLK] = (dh * up * sig * (1.0 + gate * (1.0 - sig))).astype(BF16)
-        act[y, rows, BLK:2 * BLK] = (dh * silu).astype(BF16)
-        act[y, rows, 2 * BLK:] = (silu * up).astype(BF16)
+        act[rows, pl.ds(pl.multiple_of(y * 256, 256), BLK)] = (dh * up * sig * (1.0 + gate * (1.0 - sig))).astype(BF16)
+        act[rows, pl.ds(pl.multiple_of(y * 256 + BLK, BLK), BLK)] = (dh * silu).astype(BF16)
+        hid[y, rows, :] = (silu * up).astype(BF16)
         for d in (2, 1, 3):
             go(a_copy(q, d, y))
         go(b_copy(q, 0, y, k))
+
+    def e_copy(d, src):
+        ref = hid.at[src, khalf]
+        return rc(ref, ref, e_s.at[d - 1], e_r.at[d - 1], at(dy_=d))
+
+    def f_copy(d, half):
+        ref = hid.at[yrel(-d), pl.ds(pl.multiple_of(half * HALF, HALF), HALF)]
+        return rc(ref, ref, f_s.at[d], f_r.at[d], at(dk=1))
+
+    def stage_e():
+        for d in (2, 1, 3):
+            go(e_copy(d, y))
+        go(f_copy(0, k))
+
+    def stage_f():
+        for d in (1, 3, 2):
+            e_copy(d, yrel(-d)).wait_recv()
+            go(f_copy(d, k))
+
+    def stage_k():
+        for d in (0, 1, 3, 2):
+            f_copy(d, 1 - k).wait_recv()
 
     def stage_a(q):
         for d in (1, 3, 2):
@@ -267,15 +307,12 @@
         for d in (0, 1, 3, 2):
             b_copy(q, d, yrel(-d), 1 - k).wait_recv()
 
+        lhs = jnp.concatenate([act[rows_of(q, 0), :], act[rows_of(q, 1), :]], axis=0)
+
         @pl.loop(0, DW // 256)
         def _(i):
             cs = pl.ds(pl.multiple_of(i * 256, 256), 256)
-            acc = None
-            for yb in range(NY):
-                lhs = jnp.concatenate([act[yb, rows_of(q, 0), :2 * BLK], act[yb, rows_of(q, 1), :2 * BLK]], axis=0)
-                t = nt(lhs, wgu[yb, cs, :])
-                acc = t if acc is None else acc + t
-            dxf[q % 2, :, cs] = acc
+            dxf[q % 2, :, cs] = nn(lhs, wgut[:, cs])
 
         for p in range(2):
             for xx in range(NX):
@@ -305,19 +342,27 @@
             return rc(dhp.at[:, sib], dhc, h_s.at[0], h_r.at[0], at(dk=1))
         return rc(dhs.at[d - 1], dhy.at[d - 1], h_s.at[d], h_r.at[d], at(dy_=d))
 
-    def gpair(q):
-        parts = []
-        for p in range(2):
+    def pieces_g(q):
+        parts = [pl.ds(pl.multiple_of(zrel(RHO[q][p]) * PLANE, 32), PLANE) for p in range(2)]
+
+        def rows(p):
             plane = zrel(RHO[q][p])
             G.xb_wait(RHO[q][p])
             for xx in (0, 2):
                 unslab(ga, gb, plane * NX + xx, g_all, pl.multiple_of(plane * PLANE + xx * ROWS, 2 * ROWS))
-            parts.append(pl.ds(pl.multiple_of(plane * PLANE, 32), PLANE))
-        lhs = jnp.concatenate([g_all[parts[0], :], g_all[parts[1], :]], axis=0)
-        for i in range(2):
+
+        def product(i):
+            lhs = jnp.concatenate([g_all[parts[0], :], g_all[parts[1], :]], axis=0)
             t = nt(lhs, wd[i * 256:(i + 1) * 256, :]).astype(BF16)
             dhu[parts[0], i * 256:(i + 1) * 256] = t[:PLANE]
             dhu[parts[1], i * 256:(i + 1) * 256] = t[PLANE:]
+
+        return ([functools.partial(rows, p) for p in range(2)]
+                + [functools.partial(product, i) for i in range(2)])
+
+    def gpair(q):
+        for piece in pieces_g(q):
+            piece()
 
     def permute():
         @pl.loop(0, DW // 256)
@@ -354,90 +399,109 @@
             xt[cs, :] = x_all[:, cs].astype(F32).T.astype(BF16)
 
     def weight_grads(first, last):
-        weight_grads_of(first, last)
-        cs = slice(first * BLK, last * BLK)
-        store(ggate_ref.at[:, cs], ggate_hbm.at[:, cs])
-        store(gup_ref.at[:, cs], gup_hbm.at[:, cs])
-        store(gdown_ref.at[cs], gdown_hbm.at[cs])
-
-    def weight_grads_of(first, last):
         @pl.loop(first, last)
         def _(j):
-            acc = nn(xt[...], act[j, :, :2 * BLK])
+            acc = nn(xt[...], act[:, pl.ds(pl.multiple_of(j * 256, 256), 256)])
             cs = pl.ds(pl.multiple_of(j * BLK, BLK), BLK)
             for i in range(DW // BLK):
                 f = flags[j, i].astype(F32)
                 blk = acc[i * BLK:(i + 1) * BLK] * f
                 ggate_ref[i * BLK:(i + 1) * BLK, cs] = blk[:, :BLK].astype(BF16)
                 gup_ref[i * BLK:(i + 1) * BLK, cs] = blk[:, BLK:].astype(BF16)
-            hidt[...] = act[j, :, 2 * BLK:].astype(F32).T.astype(BF16)
+
+        cs = slice(first * BLK, last * BLK)
+        store(ggate_ref.at[:, cs], ggate_hbm.at[:, cs])
+        store(gup_ref.at[:, cs], gup_hbm.at[:, cs])
+
+    def down_grads(first, last):
+        @pl.loop(first, last)
+        def _(j):
+            hidt[...] = hid[j].astype(F32).T.astype(BF16)
             acc = nn(hidt[...], dy[...])
+            cs = pl.ds(pl.multiple_of(j * BLK, BLK), BLK)
             for i in range(DW // BLK):
                 f = flags[j, i].astype(F32)
                 gdown_ref[cs, i * BLK:(i + 1) * BLK] = (acc[:, i * BLK:(i + 1) * BLK] * f).astype(BF16)
 
+        cs = slice(first * BLK, last * BLK)
+        store(gdown_ref.at[cs], gdown_hbm.at[cs])
+
+    def pieces_perm():
+        def column():
+            ocol[...] = jnp.broadcast_to(order[...].reshape(1, TOK), (BLK, TOK)).astype(F32).T
+
+        def block(q, p):
+            lane = lax.broadcasted_iota(jnp.int32, (PLANE, BLK), 1).astype(F32)
+            o = ocol[pl.ds(pl.multiple_of(zrel(RHO[q][p]) * PLANE, 32), PLANE), :]
+            for j in range(TOK // BLK):
+                perm[rows_of(q, p), j * BLK:(j + 1) * BLK] = jnp.where(o == lane + float(j * BLK), 1.0, 0.0).astype(BF16)
+
+        return [column] + [functools.partial(block, q, p) for q in range(NQ) for p in range(2)]
+
+    def pieces_transpose():
+        def one(j):
+            wgut[j * 256:(j + 1) * 256, :] = wgu[j].astype(F32).T.astype(BF16)
+
+        return [functools.partial(one, j) for j in range(NY)]
+
     def make_perm():
-        ocol[...] = jnp.broadcast_to(order[...].reshape(1, TOK), (BLK, TOK)).astype(F32).T
-        lane = lax.broadcasted_iota(jnp.int32, (PLANE, BLK), 1).astype(F32)
-        for q in range(NQ):
-            for p in range(2):
-                o = ocol[pl.ds(pl.multiple_of(zrel(RHO[q][p]) * PLANE, 32), PLANE), :]
-                for j in range(TOK // BLK):
-                    perm[rows_of(q, p), j * BLK:(j + 1) * BLK] = jnp.where(o == lane + float(j * BLK), 1.0, 0.0).astype(BF16)
+        for piece in pieces_perm():
+            piece()
+
+    def pieces_masks():
+        def wait():
+            for cp in loads[2:]:
+                cp.wait()
+
+        return [wait] + [functools.partial(masks, i, i + 1) for i in range(DW // BLK)]
 
     T.start()
     G.start()
-    make_perm()
-    T.step(1)
-    G.step(1)
-    for cp in loads[2:]:
-        cp.wait()
-    masks(0, 4)
-    T.step(2)
-    G.step(2)
-    masks(4, 8)
-    T.step(3)
-    G.step(3)
-    stage_p(0)
-    gpair(0)
-    T.step(4)
-    G.step(4)
-    stage_p(1)
-    gpair(1)
-    T.step(5)
+    T.step(1, pieces_masks()[:4])
+    G.step(1, pieces_masks()[4:])
+    T.step(2, pieces_perm()[:5])
+    G.step(2, pieces_perm()[5:])
+    T.step(3, pieces_transpose())
+    G.step(3, pieces_p(0))
+    T.step(4, pieces_g(0))
     stage_c(0)
-    stage_p(2)
-    G.step(5)
+    G.step(4, pieces_p(1))
+    T.step(5, pieces_g(1))
+    stage_c(1)
+    G.step(5, pieces_p(2))
     gpair(2)
     gpair(3)
     dh_partial()
-    stage_c(1)
     stage_p(3)
     stage_c(2)
     dh_pair()
     stage_c(3)
+    permute()
+    transpose_tokens()
     dh_total()
-    stage_y(3)
     stage_y(2)
     stage_y(1)
-    stage_a(3)
-    stage_y(0)
     stage_a(2)
-    stage_b(3)
+    stage_y(3)
     stage_a(1)
     stage_b(2)
+    stage_y(0)
+    stage_e()
+    stage_a(3)
+    stage_b(1)
     stage_a(0)
-    stage_x(3)
-    stage_b(1)
+    stage_b(3)
     stage_x(2)
     stage_b(0)
-    permute()
-    transpose_tokens()
-    weight_grads(0, 1)
     stage_x(1)
-    weight_grads(1, 2)
+    stage_f()
+    stage_x(3)
+    weight_grads(0, 2)
+    stage_k()
+    down_grads(0, 1)
     stage_x(0)
     weight_grads(2, 4)
+    down_grads(1, 4)
     for d in (1, 7, 2, 6, 3, 5, 4):
         rz_copy(d, zsrc.at[0, 0]).wait_recv()
     t = zsrc[0, 0].astype(F32)
@@ -476,17 +540,17 @@
     V = pltpu.VMEM
     n = NZ * NX
     half_slab = (n, 2 * ROWS, DW // 4)
-    sems = [5, 10]
+    sems = [5, 16]
     for _ in range(2):
         for m in (3, 8 * NP, 8, 24):
             sems += [m, m]
-    for m in (NQ, 3 * NQ, 4, 3 * NQ, 4 * NQ, 3 * NQ, 7):
+    for m in (NQ, 3 * NQ, 4, 3 * NQ, 4 * NQ, 3 * NQ, 7, 3, 4):
         sems += [m, m]
     scratch = [
         V((ROWS, DW), BF16), V((ROWS, DW), BF16), V((ROWS, DW), BF16),
         V((DW, FW), BF16), V((DW, FW), BF16), V((FW, DW), BF16),
         V((DW, FW), BF16), V((DW, FW), BF16), V((FW, DW), BF16),
-        V((NY, DW, 2 * BLK), BF16), V((FW, DW), BF16),
+        V((NY, DW, 2 * BLK), BF16), V((2 * FW, DW), BF16), V((FW, DW), BF16),
         V(half_slab, BF16), V(half_slab, BF16), V(half_slab, BF16), V(half_slab, BF16),
         V((TOK, DW), BF16), V((TOK, DW), BF16), V((TOK, DW), BF16),
         V((DW, TOK), BF16), V((TOK, TOK), BF16), V((TOK, BLK), F32),
@@ -494,7 +558,7 @@
         V((NQ, NY - 1, PLANE, 2 * BLK), BF16), V((NQ, NY - 1, PLANE, 2 * BLK), BF16),
         V((TOK, FW), BF16), V((NY, TOK, BLK), BF16), V((NY, HALF, BLK), BF16),
         V((NY - 1, HALF, BLK), BF16), V((NY - 1, HALF, BLK), BF16), V((HALF, BLK), F32),
-        V((NY, TOK, 3 * BLK), BF16), V((BLK, TOK), BF16),
+        V((TOK, 2 * FW), BF16), V((NY, TOK, BLK), BF16), V((BLK, TOK), BF16),
         V((2, 2 * PLANE, DW), F32),
         V((NQ, NX, 2) + SLAB, BF16), V((NQ, NX - 1, 2) + SLAB, BF16),
         V((NQ, 2) + SLAB, BF16), V((NZ - 1,) + SLAB, BF16),

time: 87 us -> 86.7 us (level)
  no operation moved by 1% of the time
where the time goes in v3:
time: 86.7 us; the launch traced here: 86.6 us
  Pallas kernels  85.8 us (99%)
    pallas_call x1, Pallas kernels, on_device(): pl.pallas_call(kernel, out_shape=out_shape, in_specs=[hbm, hbm, hbm, hbm,...  82.9 us
    pallas_call x1, Pallas kernels, on_device(): pl.pallas_call(copy_kernel, out_shape=out_shape, in_specs=[hbm] * 4, out_...  2.83 us

profile of v3, /device:TPU:8, one launch (start us, length us, event | category | flops | bytes accessed | tf_op | source)
XLA Modules:
  0.0 86.6 jit_solution(1548060906713629901)
XLA Ops:
  0.6 82.9 %layer_backward.1 = (bf16[24,1024]{1,0:T(8,128)(2,1)}, bf16[1024,512]{1,0:T(8,128)(2,1)}, bf16[1024,512]{1,0:T(8,128)(2,1)}, bf16[512,1024]{1,0:T(8,128)(2,1)}) custom-call(bf16[24,1024]{1,0:T(8,128)(2,1)} %tok_hbm.1, bf16[24,1024]{1,0:T(8,128)(2,1)} %go_hbm.1, bf16[1024,512]{1,0:T(8,128)(2,1)} %wg_hbm.1, bf16[1024,512]{1,0:T(8,128)(2,1)} %wu_hbm.1, ...), custom_call_target="tpu_custom_call" | custom-call | tf_op jit(solution)/shard_map/layer_backward/pallas_call | solution.py:572
  83.6 2.8 %hand_over.1 = (bf16[24,1024]{1,0:T(8,128)(2,1)}, bf16[1024,512]{1,0:T(8,128)(2,1)}, bf16[1024,512]{1,0:T(8,128)(2,1)}, bf16[512,1024]{1,0:T(8,128)(2,1)}) custom-call(bf16[24,1024]{1,0:T(8,128)(2,1)} %get-tuple-element.8.a, bf16[1024,512]{1,0:T(8,128)(2,1)} %get-tuple-element.9.b, bf16[1024,512]{1,0:T(8,128)(2,1)} %get-tuple-element.10.c, ...), custom_call_target="tpu_custom_call" | custom-call | tf_op jit(solution)/shard_map/hand_over/pallas_call | solution.py:582

commit v4 on v3

--- a/solution.py
+++ b/solution.py
@@ -35,11 +35,11 @@
 
 
 def kernel(tok_hbm, go_hbm, wg_hbm, wu_hbm, wd_hbm, flags, order,
-           gin_hbm, ggate_hbm, gup_hbm, gdown_hbm,
-           tok_ref, go_ref, gin_ref, ggate_ref, gup_ref, gdown_ref,
+           gin_ref, ggate_ref, gup_ref, gdown_ref,
+           tok_ref, go_ref,
            raw_g, raw_u, raw_d, wgu, wgut, wd, ga, gb, ta, tb, x_all, g_all, dy, xt, perm, ocol,
            part, crecv, ssend, yrecv, dhu, dhp, dhc, dhs, dhy, dht, act, hid, hidt, dxf, rsx, xrecv, zsrc, zrecv,
-           wsem, osem, gxa_s, gxa_r, gza_s, gza_r, gzb_s, gzb_r, gxb_s, gxb_r,
+           wsem, gxa_s, gxa_r, gza_s, gza_r, gzb_s, gzb_r, gxb_s, gxb_r,
            txa_s, txa_r, tza_s, tza_r, tzb_s, tzb_r, txb_s, txb_r,
            c_s, c_r, y_s, y_r, h_s, h_r, a_s, a_r, b_s, b_r, rx_s, rx_r, rz_s, rz_r, e_s, e_r, f_s, f_r):
     r = lax.axis_index("row")
@@ -81,13 +81,6 @@
                                          (wd_hbm, raw_d), (wg_hbm, raw_g), (wu_hbm, raw_u)))]
     for cp in loads:
         cp.start()
-    stores = []
-
-    def store(src, dst):
-        cp = pltpu.make_async_copy(src, dst, osem.at[len(stores)])
-        cp.start()
-        stores.append(cp)
-
     QW = DW // 4
 
     def to_slabs(ref, a, b):
@@ -409,9 +402,6 @@
                 ggate_ref[i * BLK:(i + 1) * BLK, cs] = blk[:, :BLK].astype(BF16)
                 gup_ref[i * BLK:(i + 1) * BLK, cs] = blk[:, BLK:].astype(BF16)
 
-        cs = slice(first * BLK, last * BLK)
-        store(ggate_ref.at[:, cs], ggate_hbm.at[:, cs])
-        store(gup_ref.at[:, cs], gup_hbm.at[:, cs])
 
     def down_grads(first, last):
         @pl.loop(first, last)
@@ -423,8 +413,6 @@
                 f = flags[j, i].astype(F32)
                 gdown_ref[cs, i * BLK:(i + 1) * BLK] = (acc[:, i * BLK:(i + 1) * BLK] * f).astype(BF16)
 
-        cs = slice(first * BLK, last * BLK)
-        store(gdown_ref.at[cs], gdown_hbm.at[cs])
 
     def pieces_perm():
         def column():
@@ -509,26 +497,18 @@
         t = t + zrecv[j].astype(F32)
     gin_ref[...] = jnp.concatenate([t[:ROWS], t[ROWS:]], axis=1).astype(BF16)
 
-    store(gin_ref, gin_hbm)
     for cp in started:
         cp.wait_send()
-    for cp in stores:
-        cp.wait()
-
-
-def copy_kernel(a, b, c, d, oa, ob, oc, od, va, vb, vc, vd, lsem, ssem):
-    loads, stores = [], []
-    for src, mid, dst, n in ((b, vb, ob, 4), (c, vc, oc, 4), (d, vd, od, 4), (a, va, oa, 1)):
+
+
+def copy_kernel(a, b, c, d, oa, ob, oc, od, sem):
+    stores = []
+    for src, dst, n in ((b, ob, 4), (c, oc, 4), (d, od, 4), (a, oa, 1)):
         step = src.shape[0] // n
         for i in range(n):
             rows = pl.ds(i * step, step)
-            loads.append(pltpu.make_async_copy(src.at[rows], mid.at[rows], lsem.at[len(loads)]))
-            stores.append(pltpu.make_async_copy(mid.at[rows], dst.at[rows], ssem.at[len(stores)]))
-    for cp in loads:
-        cp.start()
-    for ld, st in zip(loads, stores):
-        ld.wait()
-        st.start()
+            stores.append(pltpu.make_async_copy(src.at[rows], dst.at[rows], sem.at[len(stores)]))
+            stores[-1].start()
     for cp in stores:
         cp.wait()
 
@@ -540,15 +520,14 @@
     V = pltpu.VMEM
     n = NZ * NX
     half_slab = (n, 2 * ROWS, DW // 4)
-    sems = [5, 16]
+    sems = [5]
     for _ in range(2):
         for m in (3, 8 * NP, 8, 24):
             sems += [m, m]
     for m in (NQ, 3 * NQ, 4, 3 * NQ, 4 * NQ, 3 * NQ, 7, 3, 4):
         sems += [m, m]
     scratch = [
-        V((ROWS, DW), BF16), V((ROWS, DW), BF16), V((ROWS, DW), BF16),
-        V((DW, FW), BF16), V((DW, FW), BF16), V((FW, DW), BF16),
+        V((ROWS, DW), BF16), V((ROWS, DW), BF16),
         V((DW, FW), BF16), V((DW, FW), BF16), V((FW, DW), BF16),
         V((NY, DW, 2 * BLK), BF16), V((2 * FW, DW), BF16), V((FW, DW), BF16),
         V(half_slab, BF16), V(half_slab, BF16), V(half_slab, BF16), V(half_slab, BF16),
@@ -571,21 +550,21 @@
     )
     out = pl.pallas_call(
         kernel,
-        out_shape=out_shape,
+        out_shape=tuple(pltpu.VMEM(o.shape, o.dtype) for o in out_shape),
         in_specs=[hbm, hbm, hbm, hbm, hbm, smem, vmem],
-        out_specs=(hbm,) * 4,
+        out_specs=(vmem,) * 4,
         scratch_shapes=scratch,
         compiler_params=pltpu.CompilerParams(
-            collective_id=0, has_side_effects=True, vmem_limit_bytes=58 * 2**20),
+            collective_id=0, has_side_effects=True, vmem_limit_bytes=57 * 2**20),
         name="layer_backward",
     )(tokens, grad_out, w_gate, w_up, w_down, block_flags.T, token_order)
     return pl.pallas_call(
         copy_kernel,
         out_shape=out_shape,
-        in_specs=[hbm] * 4,
+        in_specs=[vmem] * 4,
         out_specs=(hbm,) * 4,
-        scratch_shapes=[V(o.shape, o.dtype) for o in out_shape] + [pltpu.SemaphoreType.DMA((13,))] * 2,
-        compiler_params=pltpu.CompilerParams(vmem_limit_bytes=58 * 2**20),
+        scratch_shapes=[pltpu.SemaphoreType.DMA((13,))],
+        compiler_params=pltpu.CompilerParams(vmem_limit_bytes=16 * 2**20),
         name="hand_over",
     )(*out)
 

time: 86.7 us -> 85.2 us (0.983)
  Pallas kernels: 85.8 us -> 84.3 us
    pallas_call x2, Pallas kernels: 85.8 us -> 84.3 us  [the longest x1 82.5 us: on_device(): pl.pallas_call(kernel, out_shape=tuple((pltpu.VMEM(o.shape, o.dtype) for...]
where the time goes in v4:
time: 85.2 us; the launch traced here: 85.1 us
  Pallas kernels  84.3 us (99%)
    pallas_call x1, Pallas kernels, on_device(): pl.pallas_call(kernel, out_shape=tuple((pltpu.VMEM(o.shape, o.dtype) for...  82.5 us
    pallas_call x1, Pallas kernels, on_device(): pl.pallas_call(copy_kernel, out_shape=out_shape, in_specs=[vmem] * 4, out...  1.77 us

profile of v4, /device:TPU:8, one launch (start us, length us, event | category | flops | bytes accessed | tf_op | source)
XLA Modules:
  0.0 85.1 jit_solution(15385908858597395725)
XLA Ops:
  0.6 82.5 %layer_backward.1 = (bf16[24,1024]{1,0:T(8,128)(2,1)S(1)}, bf16[1024,512]{1,0:T(8,128)(2,1)S(1)}, bf16[1024,512]{1,0:T(8,128)(2,1)S(1)}, bf16[512,1024]{1,0:T(8,128)(2,1)S(1)}) custom-call(bf16[24,1024]{1,0:T(8,128)(2,1)} %tok_hbm.1, bf16[24,1024]{1,0:T(8,128)(2,1)} %go_hbm.1, bf16[1024,512]{1,0:T(8,128)(2,1)} %wg_hbm.1, bf16[1024,512]{1,0:T(8,128)(2,1)} %wu_hbm.1, ...), custom_call_target="tpu_custom_call" | custom-call | tf_op jit(solution)/shard_map/layer_backward/pallas_call | solution.py:551
  83.1 1.8 %hand_over.1 = (bf16[24,1024]{1,0:T(8,128)(2,1)}, bf16[1024,512]{1,0:T(8,128)(2,1)}, bf16[1024,512]{1,0:T(8,128)(2,1)}, bf16[512,1024]{1,0:T(8,128)(2,1)}) custom-call(bf16[24,1024]{1,0:T(8,128)(2,1)S(1)} %get-tuple-element.8.a, bf16[1024,512]{1,0:T(8,128)(2,1)S(1)} %get-tuple-element.9.b, bf16[1024,512]{1,0:T(8,128)(2,1)S(1)} %get-tuple-element.10.c, ...), custom_call_target="tpu_custom_call" | custom-call | tf_op jit(solution)/shard_map/hand_over/pallas_call | solution.py:561

commit v5 on v4

--- a/solution.py
+++ b/solution.py
@@ -22,7 +22,7 @@
 PLANE = NX * ROWS
 RHO = ((0, -1), (1, -2), (2, -3), (3, 4))
 NQ = len(RHO)
-NP = 4
+NP = 2
 SW = NX // NP
 
 
@@ -292,9 +292,9 @@
             a_copy(q, d, yrel(-d)).wait_recv()
             go(b_copy(q, d, yrel(-d), k))
 
-    def rx_copy(q, d):
-        i = q * 3 + d - 1
-        return rc(rsx.at[q, xrel(d)], xrecv.at[q, d - 1], rx_s.at[i], rx_r.at[i], at(dx=d))
+    def rx_copy(q, p, d):
+        i = (2 * q + p) * 3 + d - 1
+        return rc(rsx.at[q, xrel(d), p], xrecv.at[q, d - 1, p], rx_s.at[i], rx_r.at[i], at(dx=d))
 
     def stage_b(q):
         for d in (0, 1, 3, 2):
@@ -307,21 +307,21 @@
             cs = pl.ds(pl.multiple_of(i * 256, 256), 256)
             dxf[q % 2, :, cs] = nn(lhs, wgut[:, cs])
 
-        for p in range(2):
+        for p in (1, 0):
             for xx in range(NX):
                 v = dxf[q % 2, p * PLANE + xx * ROWS:p * PLANE + (xx + 1) * ROWS, :]
                 rsx[q, xx, p] = jnp.concatenate([v[:, :DW // 2], v[:, DW // 2:]], axis=0).astype(BF16)
-        for d in (2, 1, 3):
-            go(rx_copy(q, d))
+            for d in (2, 1, 3):
+                go(rx_copy(q, p, d))
 
     def rz_copy(rho, src):
         i = rho % NZ - 1
         return rc(src, zrecv.at[i], rz_s.at[i], rz_r.at[i], at(dz=rho))
 
     def stage_x(q):
-        for d in (1, 3, 2):
-            rx_copy(q, d).wait_recv()
-        for p in range(2):
+        for p in (1, 0):
+            for d in (1, 3, 2):
+                rx_copy(q, p, d).wait_recv()
             t = rsx[q, x, p].astype(F32)
             for j in range(3):
                 t = t + xrecv[q, j, p].astype(F32)
@@ -483,8 +483,8 @@
     stage_b(0)
     stage_x(1)
     stage_f()
+    weight_grads(0, 2)
     stage_x(3)
-    weight_grads(0, 2)
     stage_k()
     down_grads(0, 1)
     stage_x(0)
@@ -524,7 +524,7 @@
     for _ in range(2):
         for m in (3, 8 * NP, 8, 24):
             sems += [m, m]
-    for m in (NQ, 3 * NQ, 4, 3 * NQ, 4 * NQ, 3 * NQ, 7, 3, 4):
+    for m in (NQ, 3 * NQ, 4, 3 * NQ, 4 * NQ, 6 * NQ, 7, 3, 4):
         sems += [m, m]
     scratch = [
         V((ROWS, DW), BF16), V((ROWS, DW), BF16),

time: 85.2 us -> 81.2 us (0.953)
  Pallas kernels: 84.3 us -> 80.1 us
    pallas_call x1, Pallas kernels: 82.5 us -> 78.3 us  [on_device(): pl.pallas_call(kernel, out_shape=tuple((pltpu.VMEM(o.shape, o.dtype) for...]
where the time goes in v5:
time: 81.2 us; the launch traced here: 80.7 us
  Pallas kernels  80.1 us (99%)
    pallas_call x1, Pallas kernels, on_device(): pl.pallas_call(kernel, out_shape=tuple((pltpu.VMEM(o.shape, o.dtype) for...  78.3 us
    pallas_call x1, Pallas kernels, on_device(): pl.pallas_call(copy_kernel, out_shape=out_shape, in_specs=[vmem] * 4, out...  1.77 us

profile of v5, /device:TPU:8, one launch (start us, length us, event | category | flops | bytes accessed | tf_op | source)
XLA Modules:
  0.0 80.7 jit_solution(5755238938409123150)
XLA Ops:
  0.6 78.3 %layer_backward.1 = (bf16[24,1024]{1,0:T(8,128)(2,1)S(1)}, bf16[1024,512]{1,0:T(8,128)(2,1)S(1)}, bf16[1024,512]{1,0:T(8,128)(2,1)S(1)}, bf16[512,1024]{1,0:T(8,128)(2,1)S(1)}) custom-call(bf16[24,1024]{1,0:T(8,128)(2,1)} %tok_hbm.1, bf16[24,1024]{1,0:T(8,128)(2,1)} %go_hbm.1, bf16[1024,512]{1,0:T(8,128)(2,1)} %wg_hbm.1, bf16[1024,512]{1,0:T(8,128)(2,1)} %wu_hbm.1, ...), custom_call_target="tpu_custom_call" | custom-call | tf_op jit(solution)/shard_map/layer_backward/pallas_call | solution.py:551
  78.9 1.8 %hand_over.1 = (bf16[24,1024]{1,0:T(8,128)(2,1)}, bf16[1024,512]{1,0:T(8,128)(2,1)}, bf16[1024,512]{1,0:T(8,128)(2,1)}, bf16[512,1024]{1,0:T(8,128)(2,1)}) custom-call(bf16[24,1024]{1,0:T(8,128)(2,1)S(1)} %get-tuple-element.8.a, bf16[1024,512]{1,0:T(8,128)(2,1)S(1)} %get-tuple-element.9.b, bf16[1024,512]{1,0:T(8,128)(2,1)S(1)} %get-tuple-element.10.c, ...), custom_call_target="tpu_custom_call" | custom-call | tf_op jit(solution)/shard_map/hand_over/pallas_call | solution.py:561

commit v6 on v5

--- a/solution.py
+++ b/solution.py
@@ -122,7 +122,7 @@
             return rc(ref, ref, self.xb[0].at[i], self.xb[1].at[i], at(dx=d))
 
         def xb_send(self, rel):
-            for d in (2, 1, 3):
+            for d in (1, 3, 2):
                 go(self.xb_copy(rel, d, zrel(rel) * NX + x))
 
         def xb_wait(self, rel):
@@ -130,7 +130,7 @@
                 self.xb_copy(rel, d, zrel(rel) * NX + xrel(-d)).wait_recv()
 
         def start(self):
-            for d in (2, 1, 3):
+            for d in (1, 3, 2):
                 go(self.xa_copy(d, c))
             go(self.zb_copy(1, 1, 0))
             go(self.zb_copy(-1, 1, 0))
@@ -233,7 +233,7 @@
 
     def stage_c(q):
         c_copy(q).wait_recv()
-        for d in (2, 1, 3):
+        for d in (1, 3, 2):
             ssend[q, d - 1] = (part[q, d, kplane, :].astype(F32) + crecv[q, d].astype(F32)).astype(BF16)
             go(y_copy(q, d))
 
@@ -261,7 +261,7 @@
         act[rows, pl.ds(pl.multiple_of(y * 256, 256), BLK)] = (dh * up * sig * (1.0 + gate * (1.0 - sig))).astype(BF16)
         act[rows, pl.ds(pl.multiple_of(y * 256 + BLK, BLK), BLK)] = (dh * silu).astype(BF16)
         hid[y, rows, :] = (silu * up).astype(BF16)
-        for d in (2, 1, 3):
+        for d in (1, 3, 2):
             go(a_copy(q, d, y))
         go(b_copy(q, 0, y, k))
 
@@ -274,7 +274,7 @@
         return rc(ref, ref, f_s.at[d], f_r.at[d], at(dk=1))
 
     def stage_e():
-        for d in (2, 1, 3):
+        for d in (1, 3, 2):
             go(e_copy(d, y))
         go(f_copy(0, k))
 
@@ -311,7 +311,7 @@
             for xx in range(NX):
                 v = dxf[q % 2, p * PLANE + xx * ROWS:p * PLANE + (xx + 1) * ROWS, :]
                 rsx[q, xx, p] = jnp.concatenate([v[:, :DW // 2], v[:, DW // 2:]], axis=0).astype(BF16)
-            for d in (2, 1, 3):
+            for d in (1, 3, 2):
                 go(rx_copy(q, p, d))
 
     def rz_copy(rho, src):
@@ -372,7 +372,7 @@
 
     def dh_pair():
         h_copy(0).wait_recv()
-        for d in (2, 1, 3):
+        for d in (1, 3, 2):
             yb = yrel(d)
             dhs[d - 1] = (dhp[yb, khalf, :].astype(F32) + dhc[yb].astype(F32)).astype(BF16)
             go(h_copy(d))

time: 81.2 us -> 81.7 us (level)
  no operation moved by 1% of the time
where the time goes in v6:
time: 81.7 us; the launch traced here: 80.5 us
  Pallas kernels  79.8 us (98%)
    pallas_call x1, Pallas kernels, on_device(): pl.pallas_call(kernel, out_shape=tuple((pltpu.VMEM(o.shape, o.dtype) for...  78 us
    pallas_call x1, Pallas kernels, on_device(): pl.pallas_call(copy_kernel, out_shape=out_shape, in_specs=[vmem] * 4, out...  1.77 us

profile of v6, /device:TPU:8, one launch (start us, length us, event | category | flops | bytes accessed | tf_op | source)
XLA Modules:
  0.0 80.5 jit_solution(2903404516670515161)
XLA Ops:
  0.6 78.0 %layer_backward.1 = (bf16[24,1024]{1,0:T(8,128)(2,1)S(1)}, bf16[1024,512]{1,0:T(8,128)(2,1)S(1)}, bf16[1024,512]{1,0:T(8,128)(2,1)S(1)}, bf16[512,1024]{1,0:T(8,128)(2,1)S(1)}) custom-call(bf16[24,1024]{1,0:T(8,128)(2,1)} %tok_hbm.1, bf16[24,1024]{1,0:T(8,128)(2,1)} %go_hbm.1, bf16[1024,512]{1,0:T(8,128)(2,1)} %wg_hbm.1, bf16[1024,512]{1,0:T(8,128)(2,1)} %wu_hbm.1, ...), custom_call_target="tpu_custom_call" | custom-call | tf_op jit(solution)/shard_map/layer_backward/pallas_call | solution.py:551
  78.7 1.8 %hand_over.1 = (bf16[24,1024]{1,0:T(8,128)(2,1)}, bf16[1024,512]{1,0:T(8,128)(2,1)}, bf16[1024,512]{1,0:T(8,128)(2,1)}, bf16[512,1024]{1,0:T(8,128)(2,1)}) custom-call(bf16[24,1024]{1,0:T(8,128)(2,1)S(1)} %get-tuple-element.8.a, bf16[1024,512]{1,0:T(8,128)(2,1)S(1)} %get-tuple-element.9.b, bf16[1024,512]{1,0:T(8,128)(2,1)S(1)} %get-tuple-element.10.c, ...), custom_call_target="tpu_custom_call" | custom-call | tf_op jit(solution)/shard_map/hand_over/pallas_call | solution.py:561
